TPU v7x, 256 devices: a whole 4x4x8 slice. The times are simulated.
256 devices in a mesh: ctx: 32 (over y_lo, z, core), slab: 8 (over x, y_hi).
Axes of the slice: x: 4, y: 4 (y_hi: 2, y_lo: 2; y = y_hi * 2 + y_lo), z: 8, core: 2. Of those that a mesh axis runs over, the one named last changes fastest.
Arguments:
- queries: bfloat16 [1024, 8192], P(('ctx', 'slab')), may hold values from -360 to 360
- block_lists: int32 [1024, 32], P(('ctx', 'slab')), may hold values from 0 to 63, all different within a row
- suffix_lengths: int32 [1024], P(('ctx', 'slab')), may hold values from 1 to 256, 131072 in all
- prompt_keys: bfloat16 [64, 1024, 512], P('ctx', 'slab'), may hold values from -6 to 6
- prompt_values: bfloat16 [64, 1024, 512], P('ctx', 'slab'), may hold values from -6 to 6
- suffix_keys: bfloat16 [1024, 256, 512], P(('ctx', 'slab')), may hold values from -6 to 6
- suffix_values: bfloat16 [1024, 256, 512], P(('ctx', 'slab')), may hold values from -6 to 6
Outputs:
- attended: bfloat16 [1024, 8192], P(('ctx', 'slab'))
Inputs may be any that keep to these rules, and one draw needn't show every extreme that they name: `block_lists`: each row names 32 different blocks; every block is named by some row. `suffix_lengths`: some branch has exactly 256 suffix tokens.
All inputs are finite; a program needn't handle non-finite values. No bound on the sum of `suffix_lengths` on one device may be relied on, other than what follows from the above.
Results may differ from a plain program's by a relative error of at most 0.0166.
Values may be sent and summed in bfloat16 or wider, within the bound.
A program may use at most 128 MiB of HBM per device.

v0:
```python
import jax
import jax.numpy as jnp
from jax import lax
from jax.sharding import PartitionSpec as P

HEADS = 64
KV_HEADS = 4
HEAD_DIM = 128


NEG = -1e30


def make_folder(query_heads, visible):
    score_scale = HEAD_DIM ** (-0.5)

    def run_blocks(carried, key_piece, value_piece, block_ids):

        def one_block(running, inputs):
            key_block, value_block, block_index = inputs
            sees = lax.dynamic_index_in_dim(visible, block_index, 1, keepdims=False)
            row_top, row_total, accum = running
            key_heads = key_block.reshape(-1, KV_HEADS, HEAD_DIM)
            value_heads = value_block.reshape(-1, KV_HEADS, HEAD_DIM)
            scores = (
                jnp.einsum(
                    "bgrd,tgd->bgrt", query_heads, key_heads, preferred_element_type=jnp.float32
                )
                * score_scale
            )
            usable = sees[:, None, None, None]
            newest = jnp.maximum(row_top, jnp.max(jnp.where(usable, scores, NEG), axis=-1))
            weights = jnp.where(usable, jnp.exp(scores - newest[..., None]), 0.0)
            shrink = jnp.exp(row_top - newest)
            row_total = row_total * shrink + jnp.sum(weights, axis=-1)
            accum = accum * shrink[..., None] + jnp.einsum(
                "bgrt,tgd->bgrd",
                weights.astype(jnp.bfloat16),
                value_heads,
                preferred_element_type=jnp.float32,
            )
            running = (newest, row_total, accum)
            return (running, None)

        carried, unused = lax.scan(one_block, carried, (key_piece, value_piece, block_ids))
        return carried

    return run_blocks


def shards(
    queries, block_lists, suffix_lengths, prompt_keys, prompt_values, suffix_keys, suffix_values
):
    score_scale = HEAD_DIM ** (-0.5)
    ratio = HEADS // KV_HEADS
    own_rows = queries.shape[0]
    local_blocks = prompt_keys.shape[0]
    block_total = local_blocks * lax.axis_size("ctx")
    rows_query, rows_lists = (
        lax.all_gather(queries, "slab", axis=0, tiled=True),
        lax.all_gather(block_lists, "slab", axis=0, tiled=True),
    )
    group_rows = rows_query.shape[0]
    visible = jnp.any(
        rows_lists[:, :, None] == jnp.arange(block_total, dtype=jnp.int32)[None, None, :], axis=1
    )
    query_heads = rows_query.reshape(group_rows, KV_HEADS, ratio, HEAD_DIM)
    run_blocks = make_folder(query_heads, visible)
    start_state = (
        jnp.full((group_rows, KV_HEADS, ratio), NEG, jnp.float32),
        jnp.zeros((group_rows, KV_HEADS, ratio), jnp.float32),
        jnp.zeros((group_rows, KV_HEADS, ratio, HEAD_DIM), jnp.float32),
    )
    key_piece = lax.all_gather(prompt_keys, "ctx", axis=0, tiled=True)
    value_piece = lax.all_gather(prompt_values, "ctx", axis=0, tiled=True)
    block_ids = jnp.arange(key_piece.shape[0], dtype=jnp.int32)
    prompt_top, prompt_total, prompt_accum = run_blocks(
        start_state, key_piece, value_piece, block_ids
    )
    own_query = queries.reshape(own_rows, KV_HEADS, ratio, HEAD_DIM)
    suffix_heads = suffix_keys.reshape(own_rows, -1, KV_HEADS, HEAD_DIM)
    suffix_value_heads = suffix_values.reshape(own_rows, -1, KV_HEADS, HEAD_DIM)
    suffix_scores = (
        jnp.einsum("bgrd,btgd->bgrt", own_query, suffix_heads, preferred_element_type=jnp.float32)
        * score_scale
    )
    suffix_usable = (
        jnp.arange(suffix_heads.shape[1], dtype=jnp.int32)[None, :] < suffix_lengths[:, None]
    )[:, None, None, :]
    suffix_top = jnp.max(jnp.where(suffix_usable, suffix_scores, NEG), axis=-1)
    suffix_weights = jnp.where(suffix_usable, jnp.exp(suffix_scores - suffix_top[..., None]), 0.0)
    suffix_total = jnp.sum(suffix_weights, axis=-1)
    suffix_accum = jnp.einsum(
        "bgrt,btgd->bgrd",
        suffix_weights.astype(jnp.bfloat16),
        suffix_value_heads,
        preferred_element_type=jnp.float32,
    )
    tops, totals, accums = (
        lax.all_to_all(prompt_top[None], "slab", split_axis=1, concat_axis=0, tiled=True),
        lax.all_to_all(prompt_total[None], "slab", split_axis=1, concat_axis=0, tiled=True),
        lax.all_to_all(prompt_accum[None], "slab", split_axis=1, concat_axis=0, tiled=True),
    )
    tops = jnp.concatenate([tops, suffix_top[None]], axis=0)
    totals = jnp.concatenate([totals, suffix_total[None]], axis=0)
    accums = jnp.concatenate([accums, suffix_accum[None]], axis=0)
    largest = jnp.max(tops, axis=0)
    factor = jnp.exp(tops - largest[None])
    numerator = jnp.sum(accums * factor[..., None], axis=0)
    denominator = jnp.sum(totals * factor, axis=0)
    result = numerator / denominator[..., None]
    return result.reshape(own_rows, HEADS * HEAD_DIM).astype(jnp.bfloat16)


def solution(mesh):
    return jax.shard_map(
        shards,
        mesh=mesh,
        in_specs=(
            P(("ctx", "slab"), None),
            P(("ctx", "slab"), None),
            P(("ctx", "slab")),
            P("ctx", "slab", None),
            P("ctx", "slab", None),
            P(("ctx", "slab"), None, None),
            P(("ctx", "slab"), None, None),
        ),
        out_specs=P(("ctx", "slab"), None),
        check_vma=False,
    )
```

profile of v0, /device:TPU:1, one launch (start us, length us, event | category | flops | bytes accessed | tf_op | source)
XLA Modules:
  0.0 570.7 jit_solution(9372714347761669108)
XLA Ops:
  8.0 26.1 %all-gather = s32[8,4,32]{2,1,0:T(4,128)S(1)} all-gather(s32[1,4,32]{2,1,0:T(4,128)} %bitcast.96), channel_id=1, replica_groups=mesh['ctx'=32,'slab'=8] {'slab'}, dimensions={0}, use_global_device_ids=true | all-gather | bytes 4608 | tf_op jit(solution)/shard_map/all_gather | solution.py:61
  34.5 29.3 %all-gather.1 = bf16[8,4,8192]{2,1,0:T(4,128)(2,1)S(1)} all-gather(bf16[1,4,8192]{2,1,0:T(4,128)(2,1)} %bitcast.87), channel_id=1, replica_groups=mesh['ctx'=32,'slab'=8] {'slab'}, dimensions={0}, use_global_device_ids=true | all-gather | bytes 589824 | tf_op jit(solution)/shard_map/all_gather | solution.py:60
  64.7 22.6 %all-gather.5.cloned.1.call-done = bf16[64,128,512]{2,1,0:T(8,128)(2,1)} async-done(((bf16[2,128,512]{2,1,0:T(8,128)(2,1)}), bf16[64,128,512]{2,1,0:T(8,128)(2,1)}) %all-gather.5.cloned.1.call-update) | async-done | bytes 8388624 | tf_op jit(solution)/shard_map/all_gather | solution.py:74
  87.3 74.5 %all-gather.7.cloned.1.call-done = bf16[64,128,512]{2,1,0:T(8,128)(2,1)} async-done(((bf16[2,128,512]{2,1,0:T(8,128)(2,1)}), bf16[64,128,512]{2,1,0:T(8,128)(2,1)}) %all-gather.7.cloned.1.call-update) | async-done | bytes 8388624 | tf_op jit(solution)/shard_map/all_gather | solution.py:75
  161.8 358.9 %while.15 = (s32[]{:T(128)}, f32[32,4,16]{0,2,1:T(8,128)S(1)}, f32[32,4,16]{0,2,1:T(8,128)S(1)}, f32[32,4,16,128]{3,0,2,1:T(8,128)S(1)}, s32[64]{0:T(128)S(1)}, ...) while((s32[]{:T(128)}, f32[32,4,16]{0,2,1:T(8,128)S(1)}, ...), condition=%wide.region_4.5_spmd.clone, body=%wide.region_1.4_spmd.clone.sunk | while | flops 137373696 | bytes 7209311 | solution.py:45
  164.1 1.0 constant_dynamic-slice_fusion.3
  169.7 1.0 constant_dynamic-slice_fusion.3
  175.3 1.0 constant_dynamic-slice_fusion.3
  209.0 1.0 constant_dynamic-slice_fusion.3
  214.6 1.0 constant_dynamic-slice_fusion.3
  220.2 1.0 constant_dynamic-slice_fusion.3
  225.8 1.0 constant_dynamic-slice_fusion.3
  231.4 1.0 constant_dynamic-slice_fusion.3
  237.0 1.0 constant_dynamic-slice_fusion.3
  242.6 1.0 constant_dynamic-slice_fusion.3
  248.2 1.0 constant_dynamic-slice_fusion.3
  253.8 1.0 constant_dynamic-slice_fusion.3
  259.4 1.0 constant_dynamic-slice_fusion.3
  265.1 1.0 constant_dynamic-slice_fusion.3
  315.5 1.0 constant_dynamic-slice_fusion.3
  321.1 1.0 constant_dynamic-slice_fusion.3
  326.7 1.0 constant_dynamic-slice_fusion.3
  332.4 1.0 constant_dynamic-slice_fusion.3
  338.0 1.0 constant_dynamic-slice_fusion.3
  343.6 1.0 constant_dynamic-slice_fusion.3
  349.2 1.0 constant_dynamic-slice_fusion.3
  354.8 1.0 constant_dynamic-slice_fusion.3
  360.4 1.0 constant_dynamic-slice_fusion.3
  366.0 1.0 constant_dynamic-slice_fusion.3
  371.6 1.0 constant_dynamic-slice_fusion.3
  422.1 1.0 constant_dynamic-slice_fusion.3
  427.7 1.0 constant_dynamic-slice_fusion.3
  433.3 1.0 constant_dynamic-slice_fusion.3
  438.9 1.0 constant_dynamic-slice_fusion.3
  444.5 1.0 constant_dynamic-slice_fusion.3
  450.1 1.0 constant_dynamic-slice_fusion.3
  455.7 1.0 constant_dynamic-slice_fusion.3
  461.4 1.0 constant_dynamic-slice_fusion.3
  467.0 1.0 constant_dynamic-slice_fusion.3
  472.6 1.0 constant_dynamic-slice_fusion.3
  478.2 1.0 constant_dynamic-slice_fusion.3
  521.6 6.4 %all-to-all-start.1 = ((f32[8,1,256]{2,1,0:T(1,128)}), f32[8,1,256]{2,1,0:T(1,128)S(1)}, u32[]{:S(2)}, u32[]{:S(2)}) async-start(f32[8,1,256]{2,1,0:T(1,128)} %reshape.97), calls=%async_computation.1 | async-start | bytes 16384 | tf_op jit(solution)/shard_map/all_to_all | solution.py:100
  528.8 5.7 %all-to-all-done.1 = f32[8,1,256]{2,1,0:T(1,128)S(1)} async-done(((f32[8,1,256]{2,1,0:T(1,128)}), f32[8,1,256]{2,1,0:T(1,128)S(1)}, u32[]{:S(2)}, u32[]{:S(2)}) %all-to-all-start.1) | async-done | bytes 8224 | tf_op jit(solution)/shard_map/all_to_all | solution.py:100
  534.5 3.3 all-to-all-start.2
  538.0 1.6 copy.108
  539.6 4.8 all-to-all-done.2
  544.3 3.6 all-to-all-start
  552.4 9.1 %all-to-all-done = f32[1,32,4,16,128]{4,3,2,0,1:T(8,128)S(1)} async-done(((f32[1,32,4,16,128]{4,3,2,0,1:T(8,128)}), f32[1,32,4,16,128]{4,3,2,0,1:T(8,128)S(1)}, u32[]{:S(2)}, u32[]{:S(2)}) %all-to-all-start) | async-done | bytes 1048608 | tf_op jit(solution)/shard_map/all_to_all | solution.py:102
  (718 shorter events, 220.7 us)
Async XLA Ops:
  6.5 541.4 %copy-start = (bf16[4,256,512]{2,1,0:T(8,128)(2,1)S(1)}, bf16[4,256,512]{2,1,0:T(8,128)(2,1)}, u32[]{:S(2)}) copy-start(bf16[4,256,512]{2,1,0:T(8,128)(2,1)} %param.14) | copy-start | bytes 3145732
  6.5 80.8 %all-gather.5.cloned.1.call-start = ((), (), s32[]{:S(2)}) async-start(), calls=%async_computation.3 | async-start | bytes 8650752 | tf_op jit(solution)/shard_map/all_gather | solution.py:74
  7.3 154.6 %all-gather.7.cloned.1.call-start = ((), (), s32[]{:S(2)}) async-start(), calls=%async_computation.4 | async-start | bytes 8650752 | tf_op jit(solution)/shard_map/all_gather | solution.py:75
  161.8 376.0 %copy-start.3 = (s32[4]{0:T(128)S(1)}, s32[4]{0:T(128)}, u32[]{:S(2)}) copy-start(s32[4]{0:T(128)} %param.11) | copy-start | bytes 52
  161.8 376.1 %copy-start.2 = (bf16[4,8192]{1,0:T(4,128)(2,1)S(1)}, bf16[4,8192]{1,0:T(4,128)(2,1)}, u32[]{:S(2)}) copy-start(bf16[4,8192]{1,0:T(4,128)(2,1)} %param.9) | copy-start | bytes 196612
  521.6 13.0 %all-to-all-start.1 = ((f32[8,1,256]{2,1,0:T(1,128)}), f32[8,1,256]{2,1,0:T(1,128)S(1)}, u32[]{:S(2)}, u32[]{:S(2)}) async-start(f32[8,1,256]{2,1,0:T(1,128)} %reshape.97), calls=%async_computation.1 | async-start | bytes 16384 | tf_op jit(solution)/shard_map/all_to_all | solution.py:100
  534.5 9.8 %all-to-all-start.2 = ((f32[8,1,256]{2,1,0:T(1,128)}), f32[8,1,256]{2,1,0:T(1,128)S(1)}, u32[]{:S(2)}, u32[]{:S(2)}) async-start(f32[8,1,256]{2,1,0:T(1,128)} %reshape.99), calls=%async_computation.2 | async-start | bytes 16384 | tf_op jit(solution)/shard_map/all_to_all | solution.py:101
  544.3 17.2 %all-to-all-start = ((f32[1,32,4,16,128]{4,3,2,0,1:T(8,128)}), f32[1,32,4,16,128]{4,3,2,0,1:T(8,128)S(1)}, u32[]{:S(2)}, u32[]{:S(2)}) async-start(f32[1,32,4,16,128]{4,3,2,0,1:T(8,128)} %bitcast.65), calls=%async_computation | async-start | bytes 2097152 | tf_op jit(solution)/shard_map/all_to_all | solution.py:102
  547.9 1.2 copy-start.1
Sparse Core Ops, SparseCore 0:
  9.2 78.0 all-gather.4
  89.2 72.5 all-gather.6
where the time goes:
time: 575 us; the launch traced here: 571 us
  local copies, waits for them, and re-layouts  125 us (22%)
  waiting for transfers between devices  118 us (21%)
  loops' own time  114 us (20%)
  matrix products  85.7 us (15%)
  blocking collectives  55.5 us (10%)
  other arithmetic  46.4 us (8%)
  between operations  13.6 us (2%)
  starting transfers between devices  13.4 us (2%)
    dynamic_slice x256, local copies, waits for them, and re-layouts, run_blocks(): lax.scan(one_block, carried, (key_piece, value_piece, block_ids))  117 us
    another operation x1, loops' own time, run_blocks(): lax.scan(one_block, carried, (key_piece, value_piece, block_ids))  114 us
    all_gather x1, waiting for transfers between devices, shards(): value_piece = lax.all_gather(prompt_values, 'ctx', axis=0, tiled=True)  74.5 us
    dot_general x64, matrix products, one_block(): jnp.einsum('bgrt,tgd->bgrd', weights.astype(jnp.bfloat16), value_heads, p...  52.2 us
    reduce_sum x64, other arithmetic, one_block(): row_total = row_total * shrink + jnp.sum(weights, axis=-1)  41 us
    dot_general x64, matrix products, one_block(): jnp.einsum('bgrd,tgd->bgrt', query_heads, key_heads, preferred_element_ty...  32.7 us
    all_gather x1, blocking collectives, shards(): lax.all_gather(queries, 'slab', axis=0, tiled=True)  29.3 us
    all_gather x1, blocking collectives, shards(): lax.all_gather(block_lists, 'slab', axis=0, tiled=True)  26.1 us
  transfers between devices with their start and end apart: 5, of which 5 were waited for; matrix products, arithmetic and copies ran while one was open for 1% of the time, Pallas kernels for 0%

commit v1 on v0

v1 whole, which is shorter than its diff:
```python
import jax
import jax.numpy as jnp
from jax import lax
from jax.experimental import pallas as pl
from jax.experimental.pallas import tpu as pltpu
from jax.sharding import PartitionSpec as P

HEADS = 64
KV_HEADS = 4
HEAD_DIM = 128
RATIO = HEADS // KV_HEADS
NEG = -1e30
EXP_SCALE = 1.4426950408889634 / HEAD_DIM**0.5

NX, NY, NZ = 4, 4, 8
OWN = 4
ROWS = 64
QROWS = 144
PROWS = 144
COPIES = 192

NT = (((1,), (1,)), ((), ()))
TN = (((0,), (0,)), ((), ()))
f32 = jnp.float32
bf16 = jnp.bfloat16


def combine(a, b):
    top_a, top_b = a[128:129], b[128:129]
    top = jnp.maximum(top_a, top_b)
    fa = jnp.exp2((top_a - top) * EXP_SCALE)
    fb = jnp.exp2((top_b - top) * EXP_SCALE)
    values = a[:128] * fa + b[:128] * fb
    total = (a[129:130] + a[130:131]) * fa + (b[129:130] + b[130:131]) * fb
    return values, top, total


def pack(values, top, total):
    high = total.astype(bf16).astype(f32)
    row = lax.broadcasted_iota(jnp.int32, (16, values.shape[1]), 0)
    tail = jnp.where(row == 0, top, jnp.where(row == 1, high, jnp.where(row == 2, total - high, 0.0)))
    return jnp.concatenate([values.astype(bf16), tail.astype(bf16)], axis=0)


def kernel(
    q_hbm, list_hbm, len_in, k_hbm, v_hbm, sk_hbm, sv_hbm, out_ref,
    q_in, list_in, k_in, v_in, sk_in, sv_in, qfmt, work, bits_own, bits_sib,
    qbuf, kv, vsib, scores0, scores1, part, ra, rb, rc, rz1, rz0, ry0, swap, suf_o, suf_ml,
    send_sems, recv_sems, loc_sems,
):
    ctx = lax.axis_index("ctx")
    slab = lax.axis_index("slab")
    core = lax.rem(ctx, 2)
    z = lax.rem(ctx // 2, NZ)
    x = slab // 2
    y = lax.rem(slab, 2) * 2 + ctx // (2 * NZ)

    def device(x, y, z, core):
        return (lax.rem(y, 2) * NZ + z) * 2 + core, x * 2 + y // 2

    sib = device(x, y, z, 1 - core)
    xp = device(lax.rem(x + 1, NX), y, z, core)
    xm = device(lax.rem(x + NX - 1, NX), y, z, core)
    yp = device(x, lax.rem(y + 1, NY), z, core)
    ym = device(x, lax.rem(y + NY - 1, NY), z, core)
    zp = device(x, y, lax.rem(z + 1, NZ), core)
    zm = device(x, y, lax.rem(z + NZ - 1, NZ), core)

    loads = []
    pairs = ((q_hbm, q_in), (list_hbm, list_in), (k_hbm, k_in), (v_hbm, v_in), (sk_hbm, sk_in), (sv_hbm, sv_in))
    for n, (src, dst) in enumerate(pairs):
        loads.append(pltpu.make_async_copy(src, dst, loc_sems.at[n]))
        loads[n].start()

    barrier = pltpu.get_barrier_semaphore()
    for other in (sib, xp, xm, yp, ym, zp, zm):
        pl.semaphore_signal(barrier, inc=1, device_id=other, device_id_type=pl.DeviceIdType.MESH)

    loads[0].wait()
    for half in range(2):
        for k in range(2):
            for h in range(RATIO):
                col = ((half * 2 + k) * RATIO + h) * HEAD_DIM
                work[pl.ds(h * OWN, OWN), :] = q_in[:, col : col + HEAD_DIM].astype(f32)
            qfmt[half, k] = work[0:ROWS, :].astype(bf16)
    loads[1].wait()
    lists = list_in[...]
    lane = lax.broadcasted_iota(jnp.int32, (OWN, 128), 1)
    seen = jnp.zeros((OWN, 128), f32)
    for n in range(lists.shape[1]):
        seen = jnp.where(lists[:, n : n + 1] == lane, 1.0, seen)
    for dst, at in ((bits_own, 0), (bits_sib, OWN)):
        work[0:16, :] = jnp.zeros((16, 128), f32)
        work[pl.ds(at, OWN), :] = seen
        dst[0] = work[0:16, :].astype(bf16)

    pl.semaphore_wait(barrier, 7)

    copies = {}
    done = set()

    def send(name, src, dst, to):
        n = len(copies)
        copy = pltpu.make_async_remote_copy(
            src_ref=src, dst_ref=dst, send_sem=send_sems.at[n], recv_sem=recv_sems.at[n],
            device_id=to, device_id_type=pl.DeviceIdType.MESH,
        )
        copy.start()
        copies[name] = copy

    def got(*name):
        if name not in done:
            done.add(name)
            copies[name].wait_recv()

    send(("bits",), bits_sib.at[0], bits_sib.at[1], sib)
    for k in range(2):
        send(("qsib", k), qfmt.at[1 - core, k], qbuf.at[k, 0, 0, pl.ds(ROWS, ROWS)], sib)
        qbuf[k, 0, 0, 0:ROWS, :] = qfmt[core, k]

    def own_kv(k):
        mine = pl.ds(pl.multiple_of(core * 256 + k * 128, 128), 128)
        theirs = pl.ds(pl.multiple_of((1 - core) * 256 + k * 128, 128), 128)
        for blk in range(2):
            vsib[k, 0, blk] = k_in[blk, :, theirs]
            vsib[k, 1, blk] = v_in[blk, :, theirs].T
        send(("kvsib", k), vsib.at[k], kv.at[k, 0, 1], sib)
        for blk in range(2):
            kv[k, 0, 0, 0, blk] = k_in[blk, :, mine]
            kv[k, 0, 0, 1, blk] = v_in[blk, :, mine].T

    def kv_round(k, r):
        if r == 0:
            got("kvsib", k)
            send(("kv1", k), kv.at[k, 0], kv.at[k, 1], xp)
            send(("kv2", k), kv.at[k, 0], kv.at[k, 2], xm)
        elif r == 1:
            got("kv1", k)
            send(("kv3a", k), kv.at[k, 1, 0], kv.at[k, 3, 0], xp)
            got("kv2", k)
            send(("kv3b", k), kv.at[k, 2, 1], kv.at[k, 3, 1], xm)
        else:
            got("kv3a", k)
            got("kv3b", k)

    def slot(k, dy, dz, which):
        end = QROWS if k == 0 else 2 * ROWS
        first, last = ((0, end), (0, ROWS), (ROWS, end))[which]
        return qbuf.at[k, dy, dz, pl.ds(first, last - first)]

    def y_send(k, dz):
        send(("y3", k, dz), slot(k, 0, dz, 0), slot(k, 3, dz, 0), yp)
        send(("y1", k, dz), slot(k, 0, dz, 0), slot(k, 1, dz, 0), ym)

    def y_forward(k, dz):
        got("y3", k, dz)
        send(("y2a", k, dz), slot(k, 3, dz, 1), slot(k, 2, dz, 1), yp)
        got("y1", k, dz)
        send(("y2b", k, dz), slot(k, 1, dz, 2), slot(k, 2, dz, 2), ym)

    def z_send(k, s):
        if s <= 3:
            send(("z", k, NZ - s), slot(k, 0, (NZ + 1 - s) % NZ, 0), slot(k, 0, NZ - s, 0), zp)
            send(("z", k, s), slot(k, 0, s - 1, 0), slot(k, 0, s, 0), zm)
        else:
            send(("z4a", k), slot(k, 0, 5, 1), slot(k, 0, 4, 1), zp)
            send(("z4b", k), slot(k, 0, 3, 2), slot(k, 0, 4, 2), zm)

    def q_round(k, r):
        if r == 0:
            got("qsib", k)
            if k == 0:
                got("bits")
                qbuf[0, 0, 0, 2 * ROWS : QROWS, :] = bits_own[0] + bits_sib[1]
            z_send(k, 1)
            y_send(k, 0)
        elif r <= 3:
            got("z", k, NZ - r)
            got("z", k, r)
            z_send(k, r + 1)
            y_send(k, NZ - r)
            y_send(k, r)
        elif r == 4:
            got("z4a", k)
            got("z4b", k)
            y_send(k, 4)
        if r == 1:
            y_forward(k, 0)
        elif 2 <= r <= 4:
            y_forward(k, NZ - r + 1)
            y_forward(k, r - 1)
        elif r == 5:
            y_forward(k, 4)

    def need(k, dy, p):
        for dz in (2 * p, 2 * p + 1):
            if dy == 2:
                got("y2a", k, dz)
                got("y2b", k, dz)

    def suffix(k):
        zero = jnp.zeros((ROWS, 128), bf16)
        s = None
        for half in range(2):
            which = core if half == 0 else 1 - core
            cols = pl.ds(pl.multiple_of(which * 256 + k * 128, 128), 128)
            q = qfmt[which, k]
            q = jnp.concatenate([q, zero] if half == 0 else [zero, q], axis=0)
            keys = sk_in[:, :, cols].reshape(1024, 128)
            more = lax.dot_general(keys, q, NT, preferred_element_type=f32)
            s = more if s is None else s + more
        token = lax.broadcasted_iota(jnp.int32, (1024, 128), 0)
        lane = lax.broadcasted_iota(jnp.int32, (1024, 128), 1)
        branch = lax.broadcasted_iota(jnp.int32, (1, 128), 1) & (OWN - 1)
        length = jnp.zeros((1, 128), jnp.int32)
        for b in range(OWN):
            length = jnp.where(branch == b, len_in[b], length)
        ok = ((token >> 8) == (lane & (OWN - 1))) & ((token & 255) < length)
        top = jnp.max(jnp.where(ok, s, NEG), axis=0, keepdims=True)
        w = jnp.where(ok, jnp.exp2((s - top) * EXP_SCALE), 0.0)
        total = jnp.sum(w, axis=0, keepdims=True)
        w = w.astype(bf16)
        both = []
        for half in range(2):
            which = core if half == 0 else 1 - core
            cols = pl.ds(pl.multiple_of(which * 256 + k * 128, 128), 128)
            values = sv_in[:, :, cols].reshape(1024, 128)
            both.append(lax.dot_general(values, w, TN, preferred_element_type=f32))
        lane = lax.broadcasted_iota(jnp.int32, (128, 128), 1)
        suf_o[k] = jnp.where(lane < ROWS, both[0], both[1])
        suf_ml[k, 0:1] = top
        suf_ml[k, 1:2] = total

    row = lax.broadcasted_iota(jnp.int32, (8, 128), 0)
    lane = lax.broadcasted_iota(jnp.int32, (8, 128), 1)
    block_id = jnp.where(row < 2, 2 * ctx + row, 2 * (ctx + 1 - 2 * core) + row - 2)
    pick = ((lane == block_id) & (row < 4)).astype(f32).astype(bf16)
    row = lax.broadcasted_iota(jnp.int32, (32, 256), 0)
    lane = lax.broadcasted_iota(jnp.int32, (32, 256), 1)
    spread = ((row >> 4) == (lane >> 7)) & ((row & 15) == ((lane >> 6) & 1) * OWN + (lane & (OWN - 1)))
    spread = spread.astype(f32).astype(bf16)
    ones = jnp.ones((16, 512), bf16)

    class Tile:
        def __init__(self, n, k, dy, p):
            self.k, self.dy, self.p = k, dy, p
            self.scores = (scores0, scores1)[n % 2]
            need(k, dy, p)
            self.q = qbuf[k, dy, 2 * p : 2 * p + 2, 0 : 2 * ROWS, :].reshape(256, 128)
            bits = qbuf[0, dy, 2 * p : 2 * p + 2, 2 * ROWS : QROWS, :].reshape(32, 128)
            seen = lax.dot_general(pick, bits, NT, preferred_element_type=f32).astype(bf16)
            self.seen = jnp.dot(seen, spread, preferred_element_type=f32) > 0.5
            self.top = jnp.full((1, 256), NEG, f32)
            self.acc = jnp.zeros((PROWS, 256), f32)

        def front(self, j):
            keys = jnp.concatenate([kv[self.k, xs, j // 2, 0, j % 2] for xs in range(4)], axis=0)
            s = lax.dot_general(keys, self.q, NT, preferred_element_type=f32)
            self.scores[pl.ds(j * 512, 512), :] = s
            here = jnp.max(s, axis=0, keepdims=True)
            self.top = jnp.maximum(self.top, jnp.where(self.seen[j : j + 1], here, NEG))

        def back(self, j):
            if j == 0:
                self.top = self.top.astype(bf16).astype(f32)
            values = jnp.concatenate([kv[self.k, xs, j // 2, 1, j % 2] for xs in range(4)], axis=1)
            values = jnp.concatenate([values, ones], axis=0)
            shift = jnp.where(self.seen[j : j + 1], self.top, -NEG)
            w = jnp.exp2((self.scores[pl.ds(j * 512, 512), :] - shift) * EXP_SCALE).astype(bf16)
            self.acc = self.acc + jnp.dot(values, w, preferred_element_type=f32)

        def store(self):
            packed = pack(self.acc[:128], self.top, self.acc[128:129])
            part[self.k, self.dy, self.p * 2] = packed[:, :128]
            part[self.k, self.dy, self.p * 2 + 1] = packed[:, 128:]

    def merge(k, dy, dz, *others):
        total = part[k, dy, dz].astype(f32)
        for other in others[:-1]:
            values, top, mass = combine(total, other.astype(f32))
            row = lax.broadcasted_iota(jnp.int32, (16, 128), 0)
            tail = jnp.where(row == 0, top, jnp.where(row == 1, mass, 0.0))
            total = jnp.concatenate([values, tail], axis=0)
        part[k, dy, dz] = pack(*combine(total, others[-1].astype(f32)))

    def z0(s):
        near, far = 4 - s, 4 + s
        if s >= 1:
            got("z0p", s - 1)
            for dy in range(2 if s == 1 else 4):
                merge(0, dy, near, rz0[0, s - 1, dy])
            if s < 4:
                send(("z0p", s), part.at[0, pl.ds(0, 4), near], rz0.at[0, s], zp)
            got("z0m", s - 1)
            for dy in range(2 if s == 1 else 0, 4):
                merge(0, dy, far % NZ, rz0[1, s - 1, dy])
            if s < 4:
                send(("z0m", s), part.at[0, pl.ds(0, 4), far], rz0.at[1, s], zm)
        else:
            send(("z0p", 0), part.at[0, pl.ds(0, 2), 4], rz0.at[0, 0, pl.ds(0, 2)], zp)
            send(("z0m", 0), part.at[0, pl.ds(2, 2), 4], rz0.at[1, 0, pl.ds(2, 2)], zm)

    def y0(s):
        if s == 0:
            send(("y0a",), part.at[0, 2, 0], ry0.at[0], yp)
            send(("y0c",), part.at[0, 3, 0], ry0.at[2], ym)
        elif s == 1:
            got("y0a")
            merge(0, 1, 0, ry0[0])
            send(("y0b",), part.at[0, 1, 0], ry0.at[1], yp)
        else:
            got("y0b")
            got("y0c")
            merge(0, 0, 0, ry0[1], ry0[2])

    def y1(p, s):
        a, b = 2 * p, 2 * p + 1
        if s == 0:
            send(("ra", p), part.at[1, 2, a], ra.at[p], yp)
            send(("rb", p), part.at[1, 2, b], rb.at[p], ym)
        elif s == 1:
            send(("rcb", p), part.at[1, 1, b], rc.at[0, b], yp)
        elif s == 2:
            send(("rda", p), part.at[1, 3, a], rc.at[1, a], ym)
            got("ra", p)
            merge(1, 1, a, ra[p])
            send(("rca", p), part.at[1, 1, a], rc.at[0, a], yp)
            got("rb", p)
            merge(1, 3, b, rb[p])
            send(("rdb", p), part.at[1, 3, b], rc.at[1, b], ym)
        else:
            for name in ("rcb", "rda", "rca", "rdb"):
                got(name, p)
            merge(1, 0, a, rc[0, a], rc[1, a])
            merge(1, 0, b, rc[0, b], rc[1, b])

    def z1(dz):
        if dz in (3, 2, 1, 0):
            got("z1", dz + 1)
        if dz in (6, 7, 0):
            got("z1", 7 if dz == 0 else dz - 1)
        if dz == 0:
            merge(1, 0, 0, rz1[1], rz1[7])
            return
        if dz not in (4, 5):
            merge(1, 0, dz, rz1[dz + 1 if dz < 4 else dz - 1])
        send(("z1", dz), part.at[1, 0, dz], rz1.at[dz], zp if dz <= 4 else zm)

    def finish(k):
        got("swap", k)
        lane = lax.broadcasted_iota(jnp.int32, (PROWS, 128), 1)
        a = jnp.where(lane < ROWS, part[k, 0, 0].astype(f32), swap[k].astype(f32))
        top_a, top_b = a[128:129], suf_ml[k, 0:1]
        top = jnp.maximum(top_a, top_b)
        fa = jnp.exp2((top_a - top) * EXP_SCALE)
        fb = jnp.exp2((top_b - top) * EXP_SCALE)
        total = (a[129:130] + a[130:131]) * fa + suf_ml[k, 1:2] * fb
        work[...] = ((a[:128] * fa + suf_o[k] * fb) / total).T
        for half in range(2):
            which = core if half == 0 else 1 - core
            for h in range(RATIO):
                col = pl.multiple_of((which * 2 + k) * RATIO * HEAD_DIM + h * HEAD_DIM, 128)
                rows = work[pl.ds(half * ROWS + h * OWN, OWN), :]
                out_ref[:, pl.ds(col, HEAD_DIM)] = rows.astype(bf16)

    q_round(0, 0)
    loads[2].wait()
    loads[3].wait()
    own_kv(0)
    kv_round(0, 0)
    own_kv(1)
    q_round(0, 1)
    loads[4].wait()
    loads[5].wait()
    suffix(0)
    q_round(0, 2)
    kv_round(0, 1)
    q_round(0, 3)
    q_round(0, 4)
    suffix(1)
    q_round(0, 5)
    kv_round(0, 2)

    order = [(0, dy, p) for p in (0, 3, 1, 2) for dy in (0, 1, 3, 2)]
    order += [(1, dy, p) for p in (2, 1, 3, 0) for dy in (2, 1, 3, 0)]
    after = {}

    def at(n, f, *args):
        after.setdefault(n, []).append((f, args))

    kv_round(1, 0)
    q_round(1, 0)
    at(2, q_round, 1, 1)
    at(4, q_round, 1, 2)
    at(5, kv_round, 1, 1)
    at(6, q_round, 1, 3)
    at(8, q_round, 1, 4)
    at(10, q_round, 1, 5)
    at(13, kv_round, 1, 2)
    at(15, z0, 0)
    at(18, z0, 1)
    at(21, z0, 2)
    at(24, z0, 3)
    at(27, z0, 4)
    at(27, y0, 0)
    at(28, y0, 1)
    at(30, y0, 2)
    for i, p in enumerate((2, 1, 3, 0)):
        n = 16 + 4 * i
        at(n, y1, p, 0)
        at(n + 1, y1, p, 1)
        at(n + 2, y1, p, 2)
        at(n + 4 if i < 3 else n + 3, y1, p, 3)
    at(20, z1, 4)
    at(20, z1, 5)
    at(24, z1, 3)
    at(26, z1, 2)
    at(28, z1, 6)
    at(30, z1, 7)
    at(31, z1, 1)
    at(31, z1, 0)

    tile = Tile(0, *order[0])
    for j in range(4):
        tile.front(j)
    for n in range(len(order)):
        following = Tile(n + 1, *order[n + 1]) if n + 1 < len(order) else None
        for j in range(4):
            if following is not None:
                following.front(j)
            tile.back(j)
        tile.store()
        tile = following
        for f, args in after.get(n, []):
            f(*args)
    for k in range(2):
        send(("swap", k), part.at[k, 0, 0], swap.at[k], sib)
    for k in range(2):
        finish(k)
    for name, copy in copies.items():
        if name not in done:
            copy.wait_recv()
        copy.wait_send()


def shards(
    queries, block_lists, suffix_lengths, prompt_keys, prompt_values, suffix_keys, suffix_values
):
    hbm = pl.BlockSpec(memory_space=pltpu.HBM)
    vmem = pl.BlockSpec(memory_space=pltpu.VMEM)
    smem = pl.BlockSpec(memory_space=pltpu.SMEM)
    return pl.pallas_call(
        kernel,
        out_shape=jax.ShapeDtypeStruct(queries.shape, bf16),
        in_specs=[hbm, hbm, smem, hbm, hbm, hbm, hbm],
        out_specs=vmem,
        scratch_shapes=[
            pltpu.VMEM(queries.shape, bf16),
            pltpu.VMEM(block_lists.shape, jnp.int32),
            pltpu.VMEM(prompt_keys.shape, bf16),
            pltpu.VMEM(prompt_values.shape, bf16),
            pltpu.VMEM(suffix_keys.shape, bf16),
            pltpu.VMEM(suffix_values.shape, bf16),
            pltpu.VMEM((2, 2, ROWS, 128), bf16),
            pltpu.VMEM((128, 128), f32),
            pltpu.VMEM((1, 16, 128), bf16),
            pltpu.VMEM((2, 16, 128), bf16),
            pltpu.VMEM((2, NY, NZ, QROWS, 128), bf16),
            pltpu.VMEM((2, 4, 2, 2, 2, 128, 128), bf16),
            pltpu.VMEM((2, 2, 2, 128, 128), bf16),
            pltpu.VMEM((2048, 256), f32),
            pltpu.VMEM((2048, 256), f32),
            pltpu.VMEM((2, NY, NZ, PROWS, 128), bf16),
            pltpu.VMEM((4, PROWS, 128), bf16),
            pltpu.VMEM((4, PROWS, 128), bf16),
            pltpu.VMEM((2, NZ, PROWS, 128), bf16),
            pltpu.VMEM((NZ, PROWS, 128), bf16),
            pltpu.VMEM((2, 4, 4, PROWS, 128), bf16),
            pltpu.VMEM((3, PROWS, 128), bf16),
            pltpu.VMEM((2, PROWS, 128), bf16),
            pltpu.VMEM((2, 128, 128), f32),
            pltpu.VMEM((2, 8, 128), f32),
            pltpu.SemaphoreType.DMA((COPIES,)),
            pltpu.SemaphoreType.DMA((COPIES,)),
            pltpu.SemaphoreType.DMA((6,)),
        ],
        compiler_params=pltpu.CompilerParams(
            collective_id=0, has_side_effects=True, vmem_limit_bytes=56 * 1024 * 1024
        ),
    )(queries, block_lists, suffix_lengths, prompt_keys, prompt_values, suffix_keys, suffix_values)


def solution(mesh):
    return jax.shard_map(
        shards,
        mesh=mesh,
        in_specs=(
            P(("ctx", "slab"), None),
            P(("ctx", "slab"), None),
            P(("ctx", "slab")),
            P("ctx", "slab", None),
            P("ctx", "slab", None),
            P(("ctx", "slab"), None, None),
            P(("ctx", "slab"), None, None),
        ),
        out_specs=P(("ctx", "slab"), None),
        check_vma=False,
    )
```

time: 575 us -> 90.6 us (0.16)
  local copies, waits for them, and re-layouts: 125 us -> 1.49 us
  waiting for transfers between devices: 118 us -> 0 us
  loops' own time: 114 us -> 0 us
  Pallas kernels: 0 us -> 88.9 us
  matrix products: 85.7 us -> 0 us
  blocking collectives: 55.5 us -> 0 us
  other arithmetic: 46.4 us -> 0 us
  between operations: 13.6 us -> 0.01 us
  starting transfers between devices: 13.4 us -> 0 us
    dynamic_slice x256 -> x0, local copies, waits for them, and re-layouts: 117 us -> none  [run_blocks(): lax.scan(one_block, carried, (key_piece, value_piece, block_ids))]
    another operation x1 -> x0, loops' own time: 114 us -> none  [run_blocks(): lax.scan(one_block, carried, (key_piece, value_piece, block_ids))]
    all_gather x2 -> x0, waiting for transfers between devices: 97.1 us -> none  [the longest x1 74.5 us: shards(): value_piece = lax.all_gather(prompt_values, 'ctx', axis=0, tiled=True)]
    pallas_call x0 -> x1, Pallas kernels: none -> 88.9 us  [shards(): pl.pallas_call(kernel, out_shape=jax.ShapeDtypeStruct(queries.shape, bf16...]
    dot_general x130 -> x0, matrix products: 85.7 us -> none  [the longest x64 52.2 us: one_block(): jnp.einsum('bgrt,tgd->bgrd', weights.astype(jnp.bfloat16), value_heads, p...]
    all_gather x2 -> x0, blocking collectives: 55.5 us -> none  [the longest x1 29.3 us: shards(): lax.all_gather(queries, 'slab', axis=0, tiled=True)]
    reduce_sum x67 -> x0, other arithmetic: 42.1 us -> none  [the longest x64 41 us: one_block(): row_total = row_total * shrink + jnp.sum(weights, axis=-1)]
    all_to_all x3 -> x0, waiting for transfers between devices: 19.6 us -> none  [the longest x1 9.15 us: shards(): lax.all_to_all(prompt_accum[None], 'slab', split_axis=1, concat_axis=0, t...]
  transfers between devices with their start and end apart: 5 -> 0, of which waited for: 5 -> 0; matrix products, arithmetic and copies ran while one was open for 1% -> 0% of each run, Pallas kernels for 0% -> 0%
where the time goes in v1:
time: 90.6 us; the launch traced here: 90.4 us
  Pallas kernels  88.9 us (98%)
  local copies, waits for them, and re-layouts  1.49 us (2%)
    pallas_call x1, Pallas kernels, shards(): pl.pallas_call(kernel, out_shape=jax.ShapeDtypeStruct(queries.shape, bf16...  88.9 us

profile of v1, /device:TPU:1, one launch (start us, length us, event | category | flops | bytes accessed | tf_op | source)
XLA Modules:
  0.0 90.4 jit_solution(15484688716212112757)
XLA Ops:
  0.0 88.9 %shard_map.73 = bf16[4,8192]{1,0:T(4,128)(2,1)} custom-call(bf16[4,8192]{1,0:T(4,128)(2,1)} %q_hbm.1, s32[4,32]{1,0:T(4,128)} %list_hbm.1, s32[4]{0:T(128)} %len_in.1, bf16[2,128,512]{2,1,0:T(8,128)(2,1)} %k_hbm.1, bf16[2,128,512]{2,1,0:T(8,128)(2,1)} %v_hbm.1, bf16[4,256,512]{2,1,0:T(8,128)(2,1)} %sk_hbm.1, bf16[4,256,512]{2,1,0:T(8,128)(2,1)} %sv_hbm.1), custom_call_target="tpu_custom_call" | custom-call | tf_op jit(solution)/shard_map/pallas_call | solution.py:452
  88.9 1.5 %copy.9 = bf16[4,8192]{1,0:T(4,128)(2,1)} copy(bf16[4,8192]{1,0:T(4,128)(2,1)} %shard_map.73) | data formatting | bytes 131072

commit v2 on v1

v2 whole, which is shorter than its diff:
```python
import jax
import jax.numpy as jnp
from jax import lax
from jax.experimental import pallas as pl
from jax.experimental.pallas import tpu as pltpu
from jax.sharding import PartitionSpec as P

HEADS = 64
KV_HEADS = 4
HEAD_DIM = 128
RATIO = HEADS // KV_HEADS
NEG = -1e30
EXP_SCALE = 1.4426950408889634 / HEAD_DIM**0.5

NX, NY, NZ = 4, 4, 8
OWN = 4
ROWS = 64
QROWS = 144
PROWS = 144
TILE = 512
COPIES = 192


def place(dz):
    return (dz + 1) % NZ


NT = (((1,), (1,)), ((), ()))
TN = (((0,), (0,)), ((), ()))
f32 = jnp.float32
bf16 = jnp.bfloat16


def combine(a, b):
    top_a, top_b = a[128:129], b[128:129]
    top = jnp.maximum(top_a, top_b)
    fa = jnp.exp2((top_a - top) * EXP_SCALE)
    fb = jnp.exp2((top_b - top) * EXP_SCALE)
    values = a[:128] * fa + b[:128] * fb
    total = (a[129:130] + a[130:131]) * fa + (b[129:130] + b[130:131]) * fb
    return values, top, total


def pack(values, top, total):
    high = total.astype(bf16).astype(f32)
    row = lax.broadcasted_iota(jnp.int32, (16, values.shape[1]), 0)
    tail = jnp.where(row == 0, top, jnp.where(row == 1, high, jnp.where(row == 2, total - high, 0.0)))
    return jnp.concatenate([values.astype(bf16), tail.astype(bf16)], axis=0)


def kernel(
    q_hbm, list_hbm, len_in, k_hbm, v_hbm, sk_hbm, sv_hbm, out_ref,
    q_in, list_in, k_in, v_in, sk_in, sv_in, qfmt, work, bits_own, bits_sib,
    qbuf, kv, vsib, scores0, scores1, hide, eye, part, ra, rb, rc, rz1, rz0, ry0, swap, suf_o, suf_ml,
    send_sems, recv_sems, loc_sems,
):
    ctx = lax.axis_index("ctx")
    slab = lax.axis_index("slab")
    core = lax.rem(ctx, 2)
    z = lax.rem(ctx // 2, NZ)
    x = slab // 2
    y = lax.rem(slab, 2) * 2 + ctx // (2 * NZ)

    def device(x, y, z, core):
        return (lax.rem(y, 2) * NZ + z) * 2 + core, x * 2 + y // 2

    sib = device(x, y, z, 1 - core)
    xp = device(lax.rem(x + 1, NX), y, z, core)
    xm = device(lax.rem(x + NX - 1, NX), y, z, core)
    yp = device(x, lax.rem(y + 1, NY), z, core)
    ym = device(x, lax.rem(y + NY - 1, NY), z, core)
    zp = device(x, y, lax.rem(z + 1, NZ), core)
    zm = device(x, y, lax.rem(z + NZ - 1, NZ), core)

    loads = []
    pairs = ((k_hbm, k_in), (v_hbm, v_in), (q_hbm, q_in), (list_hbm, list_in), (sk_hbm, sk_in), (sv_hbm, sv_in))
    for n, (src, dst) in enumerate(pairs):
        loads.append(pltpu.make_async_copy(src, dst, loc_sems.at[n]))
        loads[n].start()

    barrier = pltpu.get_barrier_semaphore()
    for other in (sib, xp, xm, yp, ym, zp, zm):
        pl.semaphore_signal(barrier, inc=1, device_id=other, device_id_type=pl.DeviceIdType.MESH)

    def own_kv(k):
        mine = pl.ds(pl.multiple_of(core * 256 + k * 128, 128), 128)
        theirs = pl.ds(pl.multiple_of((1 - core) * 256 + k * 128, 128), 128)
        for blk in range(2):
            vsib[k, 0, blk] = k_in[blk, :, theirs].T
            vsib[k, 1, blk] = v_in[blk, :, theirs]
            kv[k, 0, 0, 0, blk] = k_in[blk, :, mine].T
            kv[k, 0, 0, 1, blk] = v_in[blk, :, mine]

    loads[0].wait()
    loads[1].wait()
    own_kv(0)

    loads[2].wait()

    def queries(k):
        for half in range(2):
            for h in range(RATIO):
                col = ((half * 2 + k) * RATIO + h) * HEAD_DIM
                work[pl.ds(h * OWN, OWN), :] = q_in[:, col : col + HEAD_DIM].astype(f32)
            qfmt[half, k] = work[0:ROWS, :].astype(bf16)

    queries(0)
    loads[3].wait()
    lists = list_in[...]
    lane = lax.broadcasted_iota(jnp.int32, (OWN, 128), 1)
    seen = jnp.zeros((OWN, 128), f32)
    for n in range(lists.shape[1]):
        seen = jnp.where(lists[:, n : n + 1] == lane, 1.0, seen)
    for dst, first in ((bits_own, 0), (bits_sib, OWN)):
        work[0:16, :] = jnp.zeros((16, 128), f32)
        work[pl.ds(first, OWN), :] = seen
        dst[0] = work[0:16, :].astype(bf16)

    pl.semaphore_wait(barrier, 7)

    copies = {}
    done = set()

    def copy_of(name):
        n, src, dst, to = copies[name]
        return pltpu.make_async_remote_copy(
            src_ref=src, dst_ref=dst, send_sem=send_sems.at[n], recv_sem=recv_sems.at[n],
            device_id=to, device_id_type=pl.DeviceIdType.MESH,
        )

    def send(name, src, dst, to):
        copies[name] = (len(copies), src, dst, to)
        copy_of(name).start()

    def got(*name):
        if name not in done:
            done.add(name)
            copy_of(name).wait_recv()

    def exchange(k):
        send(("kvsib", k), vsib.at[k], kv.at[k, 0, 1], sib)
        send(("qsib", k), qfmt.at[1 - core, k], qbuf.at[k, 0, place(0), pl.ds(ROWS, ROWS)], sib)
        qbuf[k, 0, place(0), 0:ROWS, :] = qfmt[core, k]

    def kv_round(k, r):
        if r <= 1:
            if r == 1:
                got("kvsib", k)
            send(("kv1", k, r), kv.at[k, 0, r], kv.at[k, 1, r], xp)
            send(("kv2", k, r), kv.at[k, 0, r], kv.at[k, 2, r], xm)
        elif r == 2:
            got("kv1", k, 0)
            send(("kv3", k, 0), kv.at[k, 1, 0], kv.at[k, 3, 0], xp)
        elif r == 3:
            got("kv2", k, 1)
            send(("kv3", k, 1), kv.at[k, 2, 1], kv.at[k, 3, 1], xm)
        else:
            got("kv1", k, 1)
            got("kv2", k, 0)
            got("kv3", k, 0)
            got("kv3", k, 1)

    def slot(k, dy, dz, which):
        end = QROWS if k == 0 else 2 * ROWS
        first, last = ((0, end), (0, ROWS), (ROWS, end))[which]
        return qbuf.at[k, dy, place(dz), pl.ds(first, last - first)]

    def y_send(k, dz):
        send(("y3", k, dz), slot(k, 0, dz, 0), slot(k, 3, dz, 0), yp)
        send(("y1", k, dz), slot(k, 0, dz, 0), slot(k, 1, dz, 0), ym)

    def y_forward(k, dz):
        got("y3", k, dz)
        send(("y2a", k, dz), slot(k, 3, dz, 1), slot(k, 2, dz, 1), yp)
        got("y1", k, dz)
        send(("y2b", k, dz), slot(k, 1, dz, 2), slot(k, 2, dz, 2), ym)

    def z_send(k, s):
        if s <= 3:
            send(("z", k, NZ - s), slot(k, 0, (NZ + 1 - s) % NZ, 0), slot(k, 0, NZ - s, 0), zp)
            send(("z", k, s), slot(k, 0, s - 1, 0), slot(k, 0, s, 0), zm)
        else:
            send(("z4a", k), slot(k, 0, 5, 1), slot(k, 0, 4, 1), zp)
            send(("z4b", k), slot(k, 0, 3, 2), slot(k, 0, 4, 2), zm)

    def q_round(k, r):
        if r == 0:
            got("qsib", k)
            if k == 0:
                got("bits")
                qbuf[0, 0, place(0), 2 * ROWS : QROWS, :] = bits_own[0] + bits_sib[1]
            z_send(k, 1)
            y_send(k, 0)
        elif r <= 3:
            got("z", k, NZ - r)
            got("z", k, r)
            z_send(k, r + 1)
            y_send(k, NZ - r)
            y_send(k, r)
        elif r == 4:
            got("z4a", k)
            got("z4b", k)
            y_send(k, 4)
        if r == 1:
            y_forward(k, 0)
        elif 2 <= r <= 4:
            y_forward(k, NZ - r + 1)
            y_forward(k, r - 1)
        elif r == 5:
            y_forward(k, 4)

    def y_last(k):
        for dz in range(NZ):
            got("y2a", k, dz)
            got("y2b", k, dz)

    def suffix(k):
        zero = jnp.zeros((ROWS, 128), bf16)
        s = None
        for half in range(2):
            which = core if half == 0 else 1 - core
            cols = pl.ds(pl.multiple_of(which * 256 + k * 128, 128), 128)
            q = qfmt[which, k]
            q = jnp.concatenate([q, zero] if half == 0 else [zero, q], axis=0)
            keys = sk_in[:, :, cols].reshape(1024, 128)
            more = lax.dot_general(keys, q, NT, preferred_element_type=f32)
            s = more if s is None else s + more
        token = lax.broadcasted_iota(jnp.int32, (1024, 128), 0)
        lane = lax.broadcasted_iota(jnp.int32, (1024, 128), 1)
        branch = lax.broadcasted_iota(jnp.int32, (1, 128), 1) & (OWN - 1)
        length = jnp.zeros((1, 128), jnp.int32)
        for b in range(OWN):
            length = jnp.where(branch == b, len_in[b], length)
        ok = ((token >> 8) == (lane & (OWN - 1))) & ((token & 255) < length)
        top = jnp.max(jnp.where(ok, s, NEG), axis=0, keepdims=True)
        w = jnp.where(ok, jnp.exp2((s - top) * EXP_SCALE), 0.0)
        total = jnp.sum(w, axis=0, keepdims=True)
        w = w.astype(bf16)
        both = []
        for half in range(2):
            which = core if half == 0 else 1 - core
            cols = pl.ds(pl.multiple_of(which * 256 + k * 128, 128), 128)
            values = sv_in[:, :, cols].reshape(1024, 128)
            both.append(lax.dot_general(values, w, TN, preferred_element_type=f32))
        lane = lax.broadcasted_iota(jnp.int32, (128, 128), 1)
        suf_o[k] = jnp.where(lane < ROWS, both[0], both[1])
        suf_ml[k, 0:1] = top
        suf_ml[k, 1:2] = total

    row = lax.broadcasted_iota(jnp.int32, (128, 128), 0)
    lane = lax.broadcasted_iota(jnp.int32, (128, 128), 1)
    block_id = jnp.where(lane < 2, 2 * ctx + lane, 2 * (ctx + 1 - 2 * core) + lane - 2)
    pick = ((row == block_id) & (lane < 4)).astype(f32).astype(bf16)
    row = lax.broadcasted_iota(jnp.int32, (TILE, 64), 0)
    lane = lax.broadcasted_iota(jnp.int32, (TILE, 64), 1)
    spread = ((lane >> 4) == (row >> 7)) & ((lane & 15) == ((row >> 6) & 1) * OWN + (row & (OWN - 1)))
    spread = spread.astype(f32).astype(bf16)

    def constants():
        row = lax.broadcasted_iota(jnp.int32, (128, 128), 0)
        for j in range(4):
            hide[j] = jnp.where(row == j, NEG, 0.0).astype(bf16)
        row = lax.broadcasted_iota(jnp.int32, (PROWS, 256), 0)
        lane = lax.broadcasted_iota(jnp.int32, (PROWS, 256), 1)
        eye[...] = (row == lane).astype(f32).astype(bf16)

    class Tile:
        def __init__(self, n, k, dy, g):
            self.k, self.dy, self.slots = k, dy, pl.ds(4 * g, 4)
            self.scores = (scores0, scores1)[n % 2]

        def front(self, j):
            if j == 0:
                q = qbuf[self.k, self.dy, self.slots, 0 : 2 * ROWS, :].reshape(TILE, 128)
                bits = qbuf[0, self.dy, self.slots, 2 * ROWS : QROWS, :].reshape(64, 128)
                unseen = jnp.dot((1.0 - bits.astype(f32)).astype(bf16), pick, preferred_element_type=f32)
                unseen = jnp.dot(spread, unseen.astype(bf16), preferred_element_type=f32)
                self.q = jnp.concatenate([q, unseen.astype(bf16)], axis=1)
                self.top = jnp.full((TILE, 128), NEG, f32)
            keys = jnp.concatenate([kv[self.k, xs, j // 2, 0, j % 2] for xs in range(4)], axis=1)
            keys = jnp.concatenate([keys, jnp.concatenate([hide[j]] * 4, axis=1)], axis=0)
            s = jnp.dot(self.q, keys, preferred_element_type=f32)
            self.scores[:, pl.ds(j * 512, 512)] = s
            for c in range(0, 512, 128):
                self.top = jnp.maximum(self.top, s[:, c : c + 128])

        def back(self, j):
            if j == 0:
                top = jnp.max(self.top, axis=1, keepdims=True)
                self.top = jnp.maximum(top, 0.1 * NEG).astype(bf16).astype(f32)
                self.acc = jnp.zeros((TILE, 256), f32)
            values = jnp.concatenate([kv[self.k, xs, j // 2, 1, j % 2] for xs in range(4)], axis=0)
            values = jnp.concatenate([values, jnp.ones((512, 128), bf16)], axis=1)
            w = jnp.exp2((self.scores[:, pl.ds(j * 512, 512)] - self.top) * EXP_SCALE).astype(bf16)
            self.acc = self.acc + jnp.dot(w, values, preferred_element_type=f32)

        def store(self):
            total = self.acc[:, 128:]
            high = total.astype(bf16).astype(f32)
            lane = lax.broadcasted_iota(jnp.int32, (TILE, 128), 1)
            tail = jnp.where(lane == 0, self.top, jnp.where(lane == 1, high, jnp.where(lane == 2, total - high, 0.0)))
            packed = jnp.concatenate([self.acc[:, :128].astype(bf16), tail.astype(bf16)], axis=1)
            turned = lax.dot_general(eye[...], packed, NT, preferred_element_type=f32).astype(bf16)
            for i in range(4):
                part[self.k, self.dy, self.slots.start + i] = turned[:, i * 128 : i * 128 + 128]

    def merge(k, dy, dz, *others):
        dz = place(dz)
        others = [buf[tuple(index)] for buf, *index in others]
        total = part[k, dy, dz].astype(f32)
        for other in others[:-1]:
            values, top, mass = combine(total, other.astype(f32))
            row = lax.broadcasted_iota(jnp.int32, (16, 128), 0)
            tail = jnp.where(row == 0, top, jnp.where(row == 1, mass, 0.0))
            total = jnp.concatenate([values, tail], axis=0)
        part[k, dy, dz] = pack(*combine(total, others[-1].astype(f32)))

    def z0(s):
        near, far = 4 - s, 4 + s
        if s >= 1:
            got("z0p", s - 1)
            for dy in range(2 if s == 1 else 4):
                merge(0, dy, near, (rz0, 0, s - 1, dy))
            if s < 4:
                send(("z0p", s), part.at[0, pl.ds(0, 4), place(near)], rz0.at[0, s], zp)
            got("z0m", s - 1)
            for dy in range(2 if s == 1 else 0, 4):
                merge(0, dy, far % NZ, (rz0, 1, s - 1, dy))
            if s < 4:
                send(("z0m", s), part.at[0, pl.ds(0, 4), place(far)], rz0.at[1, s], zm)
        else:
            send(("z0p", 0), part.at[0, pl.ds(0, 2), place(4)], rz0.at[0, 0, pl.ds(0, 2)], zp)
            send(("z0m", 0), part.at[0, pl.ds(2, 2), place(4)], rz0.at[1, 0, pl.ds(2, 2)], zm)

    def y0(s):
        if s == 0:
            send(("y0a",), part.at[0, 2, place(0)], ry0.at[0], yp)
            send(("y0c",), part.at[0, 3, place(0)], ry0.at[2], ym)
        elif s == 1:
            got("y0a")
            merge(0, 1, 0, (ry0, 0))
            send(("y0b",), part.at[0, 1, place(0)], ry0.at[1], yp)
        else:
            got("y0b")
            got("y0c")
            merge(0, 0, 0, (ry0, 1), (ry0, 2))

    def y1(g, s):
        dzs = [(4 * g + i - 1) % NZ for i in range(4)]
        a, b = pl.ds(4 * g, 2), pl.ds(4 * g + 2, 2)
        if s == 0:
            send(("ra", g), part.at[1, 2, a], ra.at[g], yp)
            send(("rb", g), part.at[1, 2, b], rb.at[g], ym)
        elif s == 1:
            send(("rcb", g), part.at[1, 1, b], rc.at[0, b], yp)
        elif s == 2:
            send(("rda", g), part.at[1, 3, a], rc.at[1, a], ym)
            got("ra", g)
            for i in range(2):
                merge(1, 1, dzs[i], (ra, g, i))
            send(("rca", g), part.at[1, 1, a], rc.at[0, a], yp)
            got("rb", g)
            for i in range(2):
                merge(1, 3, dzs[2 + i], (rb, g, i))
            send(("rdb", g), part.at[1, 3, b], rc.at[1, b], ym)
        else:
            for name in ("rcb", "rda", "rca", "rdb"):
                got(name, g)
            for i in (1, 2, 0, 3) if g else (3, 0, 2, 1):
                merge(1, 0, dzs[i], (rc, 0, 4 * g + i), (rc, 1, 4 * g + i))

    def z1(dz):
        if dz in (3, 2, 1, 0):
            got("z1", dz + 1)
        if dz in (6, 7, 0):
            got("z1", 7 if dz == 0 else dz - 1)
        if dz == 0:
            merge(1, 0, 0, (rz1, 1), (rz1, 7))
            return
        if dz not in (4, 5):
            merge(1, 0, dz, (rz1, dz + 1 if dz < 4 else dz - 1))
        send(("z1", dz), part.at[1, 0, place(dz)], rz1.at[dz], zp if dz <= 4 else zm)

    def finish(k):
        got("swap", k)
        lane = lax.broadcasted_iota(jnp.int32, (PROWS, 128), 1)
        a = jnp.where(lane < ROWS, part[k, 0, place(0)].astype(f32), swap[k].astype(f32))
        top_a, top_b = a[128:129], suf_ml[k, 0:1]
        top = jnp.maximum(top_a, top_b)
        fa = jnp.exp2((top_a - top) * EXP_SCALE)
        fb = jnp.exp2((top_b - top) * EXP_SCALE)
        total = (a[129:130] + a[130:131]) * fa + suf_ml[k, 1:2] * fb
        work[...] = ((a[:128] * fa + suf_o[k] * fb) / total).T
        for half in range(2):
            which = core if half == 0 else 1 - core
            for h in range(RATIO):
                col = pl.multiple_of((which * 2 + k) * RATIO * HEAD_DIM + h * HEAD_DIM, 128)
                rows = work[pl.ds(half * ROWS + h * OWN, OWN), :]
                out_ref[:, pl.ds(col, HEAD_DIM)] = rows.astype(bf16)

    exchange(0)
    kv_round(0, 0)
    send(("bits",), bits_sib.at[0], bits_sib.at[1], sib)
    q_round(0, 0)
    kv_round(0, 1)
    own_kv(1)
    queries(1)
    constants()
    q_round(0, 1)
    loads[4].wait()
    loads[5].wait()
    suffix(0)
    q_round(0, 2)
    kv_round(0, 2)
    q_round(0, 3)
    q_round(0, 4)
    kv_round(0, 3)
    q_round(0, 5)
    exchange(1)
    suffix(1)
    kv_round(0, 4)
    kv_round(1, 0)
    q_round(1, 0)
    kv_round(1, 1)

    order = [(0, dy, g) for dy in (0, 1, 3, 2) for g in (0, 1)]
    order += [(1, dy, g) for g in (1, 0) for dy in (2, 1, 3, 0)]
    events = {}

    def at(n, f, *args):
        events.setdefault(n, []).append((f, args))

    at(0, q_round, 1, 1)
    at(1, q_round, 1, 2)
    at(1, kv_round, 1, 2)
    at(2, q_round, 1, 3)
    at(2, kv_round, 1, 3)
    at(3, q_round, 1, 4)
    at(4, q_round, 1, 5)
    at(4, y_last, 0)
    at(6, y_last, 1)
    at(6, kv_round, 1, 4)
    at(7, z0, 0)
    at(9, z0, 1)
    at(11, z0, 2)
    at(12, z0, 3)
    at(13, z0, 4)
    at(13, y0, 0)
    at(14, y0, 1)
    at(15, y0, 2)
    for i, g in enumerate((1, 0)):
        n = 8 + 4 * i
        at(n, y1, g, 0)
        at(n + 1, y1, g, 1)
        at(n + 2, y1, g, 2)
        at(n + 4 if i == 0 else n + 3, y1, g, 3)
    at(12, z1, 4)
    at(12, z1, 5)
    at(14, z1, 3)
    at(14, z1, 6)
    at(15, z1, 2)
    at(15, z1, 7)
    at(15, z1, 1)
    at(15, z1, 0)

    tile = Tile(0, *order[0])
    for j in range(4):
        tile.front(j)
    for n in range(len(order)):
        following = Tile(n + 1, *order[n + 1]) if n + 1 < len(order) else None
        for j in range(4):
            if following is not None:
                following.front(j)
            tile.back(j)
        tile.store()
        tile = following
        for f, args in events.get(n, []):
            f(*args)
    for k in range(2):
        send(("swap", k), part.at[k, 0, place(0)], swap.at[k], sib)
    for k in range(2):
        finish(k)
    for name in copies:
        if name not in done:
            copy_of(name).wait_recv()
        copy_of(name).wait_send()


def shards(
    queries, block_lists, suffix_lengths, prompt_keys, prompt_values, suffix_keys, suffix_values
):
    hbm = pl.BlockSpec(memory_space=pltpu.HBM)
    vmem = pl.BlockSpec(memory_space=pltpu.VMEM)
    smem = pl.BlockSpec(memory_space=pltpu.SMEM)
    return pl.pallas_call(
        kernel,
        out_shape=jax.ShapeDtypeStruct(queries.shape, bf16),
        in_specs=[hbm, hbm, smem, hbm, hbm, hbm, hbm],
        out_specs=vmem,
        scratch_shapes=[
            pltpu.VMEM(queries.shape, bf16),
            pltpu.VMEM(block_lists.shape, jnp.int32),
            pltpu.VMEM(prompt_keys.shape, bf16),
            pltpu.VMEM(prompt_values.shape, bf16),
            pltpu.VMEM(suffix_keys.shape, bf16),
            pltpu.VMEM(suffix_values.shape, bf16),
            pltpu.VMEM((2, 2, ROWS, 128), bf16),
            pltpu.VMEM((128, 128), f32),
            pltpu.VMEM((1, 16, 128), bf16),
            pltpu.VMEM((2, 16, 128), bf16),
            pltpu.VMEM((2, NY, NZ, QROWS, 128), bf16),
            pltpu.VMEM((2, 4, 2, 2, 2, 128, 128), bf16),
            pltpu.VMEM((2, 2, 2, 128, 128), bf16),
            pltpu.VMEM((TILE, 2048), f32),
            pltpu.VMEM((TILE, 2048), f32),
            pltpu.VMEM((4, 128, 128), bf16),
            pltpu.VMEM((PROWS, 256), bf16),
            pltpu.VMEM((2, NY, NZ, PROWS, 128), bf16),
            pltpu.VMEM((2, 2, PROWS, 128), bf16),
            pltpu.VMEM((2, 2, PROWS, 128), bf16),
            pltpu.VMEM((2, NZ, PROWS, 128), bf16),
            pltpu.VMEM((NZ, PROWS, 128), bf16),
            pltpu.VMEM((2, 4, 4, PROWS, 128), bf16),
            pltpu.VMEM((3, PROWS, 128), bf16),
            pltpu.VMEM((2, PROWS, 128), bf16),
            pltpu.VMEM((2, 128, 128), f32),
            pltpu.VMEM((2, 8, 128), f32),
            pltpu.SemaphoreType.DMA((COPIES,)),
            pltpu.SemaphoreType.DMA((COPIES,)),
            pltpu.SemaphoreType.DMA((6,)),
        ],
        compiler_params=pltpu.CompilerParams(
            collective_id=0, has_side_effects=True, vmem_limit_bytes=56 * 1024 * 1024
        ),
    )(queries, block_lists, suffix_lengths, prompt_keys, prompt_values, suffix_keys, suffix_values)


def solution(mesh):
    return jax.shard_map(
        shards,
        mesh=mesh,
        in_specs=(
            P(("ctx", "slab"), None),
            P(("ctx", "slab"), None),
            P(("ctx", "slab")),
            P("ctx", "slab", None),
            P("ctx", "slab", None),
            P(("ctx", "slab"), None, None),
            P(("ctx", "slab"), None, None),
        ),
        out_specs=P(("ctx", "slab"), None),
        check_vma=False,
    )
```

time: 90.6 us -> 95.5 us (1.054)
  Pallas kernels: 88.9 us -> 93.8 us
    pallas_call x1, Pallas kernels: 88.9 us -> 93.8 us  [shards(): pl.pallas_call(kernel, out_shape=jax.ShapeDtypeStruct(queries.shape, bf16...]
where the time goes in v2:
time: 95.5 us; the launch traced here: 95.3 us
  Pallas kernels  93.8 us (98%)
  local copies, waits for them, and re-layouts  1.49 us (2%)
    pallas_call x1, Pallas kernels, shards(): pl.pallas_call(kernel, out_shape=jax.ShapeDtypeStruct(queries.shape, bf16...  93.8 us

profile of v2, /device:TPU:1, one launch (start us, length us, event | category | flops | bytes accessed | tf_op | source)
XLA Modules:
  0.0 95.3 jit_solution(16119933449457098665)
XLA Ops:
  0.0 93.8 %shard_map.73 = bf16[4,8192]{1,0:T(4,128)(2,1)} custom-call(bf16[4,8192]{1,0:T(4,128)(2,1)} %q_hbm.1, s32[4,32]{1,0:T(4,128)} %list_hbm.1, s32[4]{0:T(128)} %len_in.1, bf16[2,128,512]{2,1,0:T(8,128)(2,1)} %k_hbm.1, bf16[2,128,512]{2,1,0:T(8,128)(2,1)} %v_hbm.1, bf16[4,256,512]{2,1,0:T(8,128)(2,1)} %sk_hbm.1, bf16[4,256,512]{2,1,0:T(8,128)(2,1)} %sv_hbm.1), custom_call_target="tpu_custom_call" | custom-call | tf_op jit(solution)/shard_map/pallas_call | solution.py:495
  93.8 1.5 %copy.9 = bf16[4,8192]{1,0:T(4,128)(2,1)} copy(bf16[4,8192]{1,0:T(4,128)(2,1)} %shard_map.73) | data formatting | bytes 131072

commit v3 on v1

--- a/solution.py
+++ b/solution.py
@@ -15,7 +15,7 @@
 NX, NY, NZ = 4, 4, 8
 OWN = 4
 ROWS = 64
-QROWS = 144
+QROWS = 272
 PROWS = 144
 COPIES = 192
 
@@ -42,12 +42,7 @@
     return jnp.concatenate([values.astype(bf16), tail.astype(bf16)], axis=0)
 
 
-def kernel(
-    q_hbm, list_hbm, len_in, k_hbm, v_hbm, sk_hbm, sv_hbm, out_ref,
-    q_in, list_in, k_in, v_in, sk_in, sv_in, qfmt, work, bits_own, bits_sib,
-    qbuf, kv, vsib, scores0, scores1, part, ra, rb, rc, rz1, rz0, ry0, swap, suf_o, suf_ml,
-    send_sems, recv_sems, loc_sems,
-):
+def position():
     ctx = lax.axis_index("ctx")
     slab = lax.axis_index("slab")
     core = lax.rem(ctx, 2)
@@ -66,6 +61,42 @@
     zp = device(x, y, lax.rem(z + 1, NZ), core)
     zm = device(x, y, lax.rem(z + NZ - 1, NZ), core)
 
+    return ctx, core, sib, xp, xm, yp, ym, zp, zm
+
+
+def sender(send_sems, recv_sems):
+    copies = {}
+    done = set()
+
+    def send(name, src, dst, to):
+        n = len(copies)
+        copy = pltpu.make_async_remote_copy(
+            src_ref=src, dst_ref=dst, send_sem=send_sems.at[n], recv_sem=recv_sems.at[n],
+            device_id=to, device_id_type=pl.DeviceIdType.MESH,
+        )
+        copy.start()
+        copies[name] = copy
+
+    def got(*name):
+        if name not in done:
+            done.add(name)
+            copies[name].wait_recv()
+
+    def close():
+        for name, copy in copies.items():
+            if name not in done:
+                copy.wait_recv()
+            copy.wait_send()
+
+    return send, got, close
+
+
+def gather_kernel(
+    q_hbm, list_hbm, len_in, k_hbm, v_hbm, sk_hbm, sv_hbm, q_out, kv_out, suf_o, suf_ml,
+    q_in, list_in, k_in, v_in, sk_in, sv_in, qfmt, work, bits_own, bits_sib,
+    qbuf, kv, vsib, send_sems, recv_sems, loc_sems,
+):
+    ctx, core, sib, xp, xm, yp, ym, zp, zm = position()
     loads = []
     pairs = ((q_hbm, q_in), (list_hbm, list_in), (k_hbm, k_in), (v_hbm, v_in), (sk_hbm, sk_in), (sv_hbm, sv_in))
     for n, (src, dst) in enumerate(pairs):
@@ -96,107 +127,86 @@
 
     pl.semaphore_wait(barrier, 7)
 
-    copies = {}
-    done = set()
-
-    def send(name, src, dst, to):
-        n = len(copies)
-        copy = pltpu.make_async_remote_copy(
-            src_ref=src, dst_ref=dst, send_sem=send_sems.at[n], recv_sem=recv_sems.at[n],
-            device_id=to, device_id_type=pl.DeviceIdType.MESH,
-        )
-        copy.start()
-        copies[name] = copy
-
-    def got(*name):
-        if name not in done:
-            done.add(name)
-            copies[name].wait_recv()
+    send, got, close = sender(send_sems, recv_sems)
 
     send(("bits",), bits_sib.at[0], bits_sib.at[1], sib)
     for k in range(2):
-        send(("qsib", k), qfmt.at[1 - core, k], qbuf.at[k, 0, 0, pl.ds(ROWS, ROWS)], sib)
-        qbuf[k, 0, 0, 0:ROWS, :] = qfmt[core, k]
-
-    def own_kv(k):
+        send(("qsib", k), qfmt.at[1 - core, k], qbuf.at[0, 0, pl.ds((2 * k + 1) * ROWS, ROWS)], sib)
+        qbuf[0, 0, 2 * k * ROWS : (2 * k + 1) * ROWS, :] = qfmt[core, k]
+
+    loads[2].wait()
+    loads[3].wait()
+    for k in range(2):
         mine = pl.ds(pl.multiple_of(core * 256 + k * 128, 128), 128)
         theirs = pl.ds(pl.multiple_of((1 - core) * 256 + k * 128, 128), 128)
         for blk in range(2):
             vsib[k, 0, blk] = k_in[blk, :, theirs]
             vsib[k, 1, blk] = v_in[blk, :, theirs].T
-        send(("kvsib", k), vsib.at[k], kv.at[k, 0, 1], sib)
-        for blk in range(2):
-            kv[k, 0, 0, 0, blk] = k_in[blk, :, mine]
-            kv[k, 0, 0, 1, blk] = v_in[blk, :, mine].T
-
-    def kv_round(k, r):
+            kv[0, 0, k, 0, blk] = k_in[blk, :, mine]
+            kv[0, 0, k, 1, blk] = v_in[blk, :, mine].T
+    send(("kvsib",), vsib, kv.at[0, 1], sib)
+
+    def kv_round(r):
         if r == 0:
-            got("kvsib", k)
-            send(("kv1", k), kv.at[k, 0], kv.at[k, 1], xp)
-            send(("kv2", k), kv.at[k, 0], kv.at[k, 2], xm)
+            got("kvsib")
+            send(("kv1",), kv.at[0], kv.at[1], xp)
+            send(("kv2",), kv.at[0], kv.at[2], xm)
         elif r == 1:
-            got("kv1", k)
-            send(("kv3a", k), kv.at[k, 1, 0], kv.at[k, 3, 0], xp)
-            got("kv2", k)
-            send(("kv3b", k), kv.at[k, 2, 1], kv.at[k, 3, 1], xm)
+            got("kv1")
+            send(("kv3a",), kv.at[1, 0], kv.at[3, 0], xp)
+            got("kv2")
+            send(("kv3b",), kv.at[2, 1], kv.at[3, 1], xm)
         else:
-            got("kv3a", k)
-            got("kv3b", k)
-
-    def slot(k, dy, dz, which):
-        end = QROWS if k == 0 else 2 * ROWS
-        first, last = ((0, end), (0, ROWS), (ROWS, end))[which]
-        return qbuf.at[k, dy, dz, pl.ds(first, last - first)]
-
-    def y_send(k, dz):
-        send(("y3", k, dz), slot(k, 0, dz, 0), slot(k, 3, dz, 0), yp)
-        send(("y1", k, dz), slot(k, 0, dz, 0), slot(k, 1, dz, 0), ym)
-
-    def y_forward(k, dz):
-        got("y3", k, dz)
-        send(("y2a", k, dz), slot(k, 3, dz, 1), slot(k, 2, dz, 1), yp)
-        got("y1", k, dz)
-        send(("y2b", k, dz), slot(k, 1, dz, 2), slot(k, 2, dz, 2), ym)
-
-    def z_send(k, s):
+            got("kv3a")
+            got("kv3b")
+
+    def slot(dy, dz, which):
+        first, last = ((0, QROWS), (0, 2 * ROWS), (2 * ROWS, QROWS))[which]
+        return qbuf.at[dy, dz, pl.ds(first, last - first)]
+
+    def y_send(dz):
+        send(("y3", dz), slot(0, dz, 0), slot(3, dz, 0), yp)
+        send(("y1", dz), slot(0, dz, 0), slot(1, dz, 0), ym)
+
+    def y_forward(dz):
+        got("y3", dz)
+        send(("y2a", dz), slot(3, dz, 1), slot(2, dz, 1), yp)
+        got("y1", dz)
+        send(("y2b", dz), slot(1, dz, 2), slot(2, dz, 2), ym)
+
+    def z_send(s):
         if s <= 3:
-            send(("z", k, NZ - s), slot(k, 0, (NZ + 1 - s) % NZ, 0), slot(k, 0, NZ - s, 0), zp)
-            send(("z", k, s), slot(k, 0, s - 1, 0), slot(k, 0, s, 0), zm)
+            send(("z", NZ - s), slot(0, (NZ + 1 - s) % NZ, 0), slot(0, NZ - s, 0), zp)
+            send(("z", s), slot(0, s - 1, 0), slot(0, s, 0), zm)
         else:
-            send(("z4a", k), slot(k, 0, 5, 1), slot(k, 0, 4, 1), zp)
-            send(("z4b", k), slot(k, 0, 3, 2), slot(k, 0, 4, 2), zm)
-
-    def q_round(k, r):
+            send(("z4a",), slot(0, 5, 1), slot(0, 4, 1), zp)
+            send(("z4b",), slot(0, 3, 2), slot(0, 4, 2), zm)
+
+    def q_round(r):
         if r == 0:
-            got("qsib", k)
-            if k == 0:
-                got("bits")
-                qbuf[0, 0, 0, 2 * ROWS : QROWS, :] = bits_own[0] + bits_sib[1]
-            z_send(k, 1)
-            y_send(k, 0)
+            got("qsib", 0)
+            got("qsib", 1)
+            got("bits")
+            qbuf[0, 0, 4 * ROWS : QROWS, :] = bits_own[0] + bits_sib[1]
+            z_send(1)
+            y_send(0)
         elif r <= 3:
-            got("z", k, NZ - r)
-            got("z", k, r)
-            z_send(k, r + 1)
-            y_send(k, NZ - r)
-            y_send(k, r)
+            got("z", NZ - r)
+            got("z", r)
+            z_send(r + 1)
+            y_send(NZ - r)
+            y_send(r)
         elif r == 4:
-            got("z4a", k)
-            got("z4b", k)
-            y_send(k, 4)
+            got("z4a")
+            got("z4b")
+            y_send(4)
         if r == 1:
-            y_forward(k, 0)
+            y_forward(0)
         elif 2 <= r <= 4:
-            y_forward(k, NZ - r + 1)
-            y_forward(k, r - 1)
+            y_forward(NZ - r + 1)
+            y_forward(r - 1)
         elif r == 5:
-            y_forward(k, 4)
-
-    def need(k, dy, p):
-        for dz in (2 * p, 2 * p + 1):
-            if dy == 2:
-                got("y2a", k, dz)
-                got("y2b", k, dz)
+            y_forward(4)
 
     def suffix(k):
         zero = jnp.zeros((ROWS, 128), bf16)
@@ -231,6 +241,48 @@
         suf_ml[k, 0:1] = top
         suf_ml[k, 1:2] = total
 
+    q_round(0)
+    kv_round(0)
+    q_round(1)
+    q_round(2)
+    loads[4].wait()
+    loads[5].wait()
+    suffix(0)
+    q_round(3)
+    kv_round(1)
+    q_round(4)
+    suffix(1)
+    q_round(5)
+    kv_round(2)
+    close()
+    stores = [
+        pltpu.make_async_copy(qbuf, q_out, loc_sems.at[0]),
+        pltpu.make_async_copy(kv, kv_out, loc_sems.at[1]),
+    ]
+    for copy in stores:
+        copy.start()
+    for copy in stores:
+        copy.wait()
+
+
+def attend_kernel(
+    q_hbm, kv_hbm, suf_o, suf_ml, out_ref,
+    qbuf, kv, work, scores0, scores1, part, ra, rb, rc, rz1, rz0, ry0, swap, send_sems, recv_sems, loc_sems,
+):
+    ctx, core, sib, xp, xm, yp, ym, zp, zm = position()
+    loads = [
+        pltpu.make_async_copy(q_hbm, qbuf, loc_sems.at[0]),
+        pltpu.make_async_copy(kv_hbm, kv, loc_sems.at[1]),
+    ]
+    for copy in loads:
+        copy.start()
+    barrier = pltpu.get_barrier_semaphore()
+    for other in (sib, yp, ym, zp, zm):
+        pl.semaphore_signal(barrier, inc=1, device_id=other, device_id_type=pl.DeviceIdType.MESH)
+    send, got, close = sender(send_sems, recv_sems)
+    for copy in loads:
+        copy.wait()
+
     row = lax.broadcasted_iota(jnp.int32, (8, 128), 0)
     lane = lax.broadcasted_iota(jnp.int32, (8, 128), 1)
     block_id = jnp.where(row < 2, 2 * ctx + row, 2 * (ctx + 1 - 2 * core) + row - 2)
@@ -245,16 +297,15 @@
         def __init__(self, n, k, dy, p):
             self.k, self.dy, self.p = k, dy, p
             self.scores = (scores0, scores1)[n % 2]
-            need(k, dy, p)
-            self.q = qbuf[k, dy, 2 * p : 2 * p + 2, 0 : 2 * ROWS, :].reshape(256, 128)
-            bits = qbuf[0, dy, 2 * p : 2 * p + 2, 2 * ROWS : QROWS, :].reshape(32, 128)
+            self.q = qbuf[dy, 2 * p : 2 * p + 2, 2 * k * ROWS : 2 * (k + 1) * ROWS, :].reshape(256, 128)
+            bits = qbuf[dy, 2 * p : 2 * p + 2, 4 * ROWS : QROWS, :].reshape(32, 128)
             seen = lax.dot_general(pick, bits, NT, preferred_element_type=f32).astype(bf16)
             self.seen = jnp.dot(seen, spread, preferred_element_type=f32) > 0.5
             self.top = jnp.full((1, 256), NEG, f32)
             self.acc = jnp.zeros((PROWS, 256), f32)
 
         def front(self, j):
-            keys = jnp.concatenate([kv[self.k, xs, j // 2, 0, j % 2] for xs in range(4)], axis=0)
+            keys = jnp.concatenate([kv[xs, j // 2, self.k, 0, j % 2] for xs in range(4)], axis=0)
             s = lax.dot_general(keys, self.q, NT, preferred_element_type=f32)
             self.scores[pl.ds(j * 512, 512), :] = s
             here = jnp.max(s, axis=0, keepdims=True)
@@ -263,7 +314,7 @@
         def back(self, j):
             if j == 0:
                 self.top = self.top.astype(bf16).astype(f32)
-            values = jnp.concatenate([kv[self.k, xs, j // 2, 1, j % 2] for xs in range(4)], axis=1)
+            values = jnp.concatenate([kv[xs, j // 2, self.k, 1, j % 2] for xs in range(4)], axis=1)
             values = jnp.concatenate([values, ones], axis=0)
             shift = jnp.where(self.seen[j : j + 1], self.top, -NEG)
             w = jnp.exp2((self.scores[pl.ds(j * 512, 512), :] - shift) * EXP_SCALE).astype(bf16)
@@ -363,24 +414,6 @@
                 rows = work[pl.ds(half * ROWS + h * OWN, OWN), :]
                 out_ref[:, pl.ds(col, HEAD_DIM)] = rows.astype(bf16)
 
-    q_round(0, 0)
-    loads[2].wait()
-    loads[3].wait()
-    own_kv(0)
-    kv_round(0, 0)
-    own_kv(1)
-    q_round(0, 1)
-    loads[4].wait()
-    loads[5].wait()
-    suffix(0)
-    q_round(0, 2)
-    kv_round(0, 1)
-    q_round(0, 3)
-    q_round(0, 4)
-    suffix(1)
-    q_round(0, 5)
-    kv_round(0, 2)
-
     order = [(0, dy, p) for p in (0, 3, 1, 2) for dy in (0, 1, 3, 2)]
     order += [(1, dy, p) for p in (2, 1, 3, 0) for dy in (2, 1, 3, 0)]
     after = {}
@@ -388,15 +421,6 @@
     def at(n, f, *args):
         after.setdefault(n, []).append((f, args))
 
-    kv_round(1, 0)
-    q_round(1, 0)
-    at(2, q_round, 1, 1)
-    at(4, q_round, 1, 2)
-    at(5, kv_round, 1, 1)
-    at(6, q_round, 1, 3)
-    at(8, q_round, 1, 4)
-    at(10, q_round, 1, 5)
-    at(13, kv_round, 1, 2)
     at(15, z0, 0)
     at(18, z0, 1)
     at(21, z0, 2)
@@ -431,16 +455,15 @@
             tile.back(j)
         tile.store()
         tile = following
+        if n == 14:
+            pl.semaphore_wait(barrier, 5)
         for f, args in after.get(n, []):
             f(*args)
     for k in range(2):
         send(("swap", k), part.at[k, 0, 0], swap.at[k], sib)
     for k in range(2):
         finish(k)
-    for name, copy in copies.items():
-        if name not in done:
-            copy.wait_recv()
-        copy.wait_send()
+    close()
 
 
 def shards(
@@ -449,11 +472,17 @@
     hbm = pl.BlockSpec(memory_space=pltpu.HBM)
     vmem = pl.BlockSpec(memory_space=pltpu.VMEM)
     smem = pl.BlockSpec(memory_space=pltpu.SMEM)
-    return pl.pallas_call(
-        kernel,
-        out_shape=jax.ShapeDtypeStruct(queries.shape, bf16),
+    q_shape, kv_shape = (NY, NZ, QROWS, 128), (4, 2, 2, 2, 2, 128, 128)
+    gathered = pl.pallas_call(
+        gather_kernel,
+        out_shape=[
+            jax.ShapeDtypeStruct(q_shape, bf16),
+            jax.ShapeDtypeStruct(kv_shape, bf16),
+            jax.ShapeDtypeStruct((2, 128, 128), f32),
+            jax.ShapeDtypeStruct((2, 8, 128), f32),
+        ],
         in_specs=[hbm, hbm, smem, hbm, hbm, hbm, hbm],
-        out_specs=vmem,
+        out_specs=[hbm, hbm, vmem, vmem],
         scratch_shapes=[
             pltpu.VMEM(queries.shape, bf16),
             pltpu.VMEM(block_lists.shape, jnp.int32),
@@ -465,9 +494,26 @@
             pltpu.VMEM((128, 128), f32),
             pltpu.VMEM((1, 16, 128), bf16),
             pltpu.VMEM((2, 16, 128), bf16),
-            pltpu.VMEM((2, NY, NZ, QROWS, 128), bf16),
-            pltpu.VMEM((2, 4, 2, 2, 2, 128, 128), bf16),
+            pltpu.VMEM(q_shape, bf16),
+            pltpu.VMEM(kv_shape, bf16),
             pltpu.VMEM((2, 2, 2, 128, 128), bf16),
+            pltpu.SemaphoreType.DMA((COPIES,)),
+            pltpu.SemaphoreType.DMA((COPIES,)),
+            pltpu.SemaphoreType.DMA((6,)),
+        ],
+        compiler_params=pltpu.CompilerParams(
+            collective_id=0, has_side_effects=True, vmem_limit_bytes=56 * 1024 * 1024
+        ),
+    )(queries, block_lists, suffix_lengths, prompt_keys, prompt_values, suffix_keys, suffix_values)
+    return pl.pallas_call(
+        attend_kernel,
+        out_shape=jax.ShapeDtypeStruct(queries.shape, bf16),
+        in_specs=[hbm, hbm, vmem, vmem],
+        out_specs=vmem,
+        scratch_shapes=[
+            pltpu.VMEM(q_shape, bf16),
+            pltpu.VMEM(kv_shape, bf16),
+            pltpu.VMEM((128, 128), f32),
             pltpu.VMEM((2048, 256), f32),
             pltpu.VMEM((2048, 256), f32),
             pltpu.VMEM((2, NY, NZ, PROWS, 128), bf16),
@@ -478,16 +524,14 @@
             pltpu.VMEM((2, 4, 4, PROWS, 128), bf16),
             pltpu.VMEM((3, PROWS, 128), bf16),
             pltpu.VMEM((2, PROWS, 128), bf16),
-            pltpu.VMEM((2, 128, 128), f32),
-            pltpu.VMEM((2, 8, 128), f32),
             pltpu.SemaphoreType.DMA((COPIES,)),
             pltpu.SemaphoreType.DMA((COPIES,)),
-            pltpu.SemaphoreType.DMA((6,)),
+            pltpu.SemaphoreType.DMA((2,)),
         ],
         compiler_params=pltpu.CompilerParams(
-            collective_id=0, has_side_effects=True, vmem_limit_bytes=56 * 1024 * 1024
+            collective_id=1, has_side_effects=True, vmem_limit_bytes=56 * 1024 * 1024
         ),
-    )(queries, block_lists, suffix_lengths, prompt_keys, prompt_values, suffix_keys, suffix_values)
+    )(*gathered)
 
 
 def solution(mesh):

time: 90.6 us -> 101 us (1.11)
  Pallas kernels: 88.9 us -> 99.5 us
    pallas_call x1 -> x2, Pallas kernels: 88.9 us -> 99.5 us  [the longest x1 60.1 us: shards(): pl.pallas_call(attend_kernel, out_shape=jax.ShapeDtypeStruct(queries.shap...]
where the time goes in v3:
time: 101 us
  Pallas kernels  99.5 us (99%)
  local copies, waits for them, and re-layouts  1.49 us (1%)
    pallas_call x1, Pallas kernels, shards(): pl.pallas_call(attend_kernel, out_shape=jax.ShapeDtypeStruct(queries.shap...  60.1 us
    pallas_call x1, Pallas kernels, shards(): pl.pallas_call(gather_kernel, out_shape=[jax.ShapeDtypeStruct(q_shape, bf...  39.4 us

profile of v3, /device:TPU:1, one launch (start us, length us, event | category | flops | bytes accessed | tf_op | source)
XLA Modules:
  0.0 101.0 jit_solution(7736981514525273258)
XLA Ops:
  0.0 39.4 %shard_map.73 = (bf16[4,8,272,128]{3,2,1,0:T(8,128)(2,1)}, bf16[4,2,2,2,2,128,128]{6,5,4,3,2,1,0:T(8,128)(2,1)}, f32[2,128,128]{2,1,0:T(8,128)}, f32[2,8,128]{2,1,0:T(8,128)}) custom-call(bf16[4,8192]{1,0:T(4,128)(2,1)} %q_hbm.1, s32[4,32]{1,0:T(4,128)} %list_hbm.1, s32[4]{0:T(128)} %len_in.1, bf16[2,128,512]{2,1,0:T(8,128)(2,1)} %k_hbm.1, ...), custom_call_target="tpu_custom_call" | custom-call | tf_op jit(solution)/shard_map/pallas_call | solution.py:476
  39.4 60.1 %shard_map.74 = bf16[4,8192]{1,0:T(4,128)(2,1)} custom-call(bf16[4,8,272,128]{3,2,1,0:T(8,128)(2,1)} %get-tuple-element.9.q_hbm, bf16[4,2,2,2,2,128,128]{6,5,4,3,2,1,0:T(8,128)(2,1)} %get-tuple-element.10.kv_hbm, f32[2,128,128]{2,1,0:T(8,128)} %get-tuple-element.11.suf_o, f32[2,8,128]{2,1,0:T(8,128)} %get-tuple-element.12.suf_ml), custom_call_target="tpu_custom_call" | custom-call | tf_op jit(solution)/shard_map/pallas_call | solution.py:508
  99.5 1.5 %copy.9 = bf16[4,8192]{1,0:T(4,128)(2,1)} copy(bf16[4,8192]{1,0:T(4,128)(2,1)} %shard_map.74) | data formatting | bytes 131072

commit v4 on v2

v4 whole, which is shorter than its diff:
```python
import jax
import jax.numpy as jnp
from jax import lax
from jax.experimental import pallas as pl
from jax.experimental.pallas import tpu as pltpu
from jax.sharding import PartitionSpec as P

HEADS = 64
KV_HEADS = 4
HEAD_DIM = 128
RATIO = HEADS // KV_HEADS
NEG = -1e30
EXP_SCALE = 1.4426950408889634 / HEAD_DIM**0.5

NX, NY, NZ = 4, 4, 8
OWN = 4
ROWS = 64
QROWS = 80
PROWS = 144
TILE = 1024
COPIES = 192


def place(dz):
    return (dz + 1) % NZ


NT = (((1,), (1,)), ((), ()))
TN = (((0,), (0,)), ((), ()))
f32 = jnp.float32
bf16 = jnp.bfloat16


def combine(a, b):
    top_a, top_b = a[128:129], b[128:129]
    top = jnp.maximum(top_a, top_b)
    fa = jnp.exp2((top_a - top) * EXP_SCALE)
    fb = jnp.exp2((top_b - top) * EXP_SCALE)
    values = a[:128] * fa + b[:128] * fb
    total = (a[129:130] + a[130:131]) * fa + (b[129:130] + b[130:131]) * fb
    return values, top, total


def pack(values, top, total):
    high = total.astype(bf16).astype(f32)
    row = lax.broadcasted_iota(jnp.int32, (16, values.shape[1]), 0)
    tail = jnp.where(row == 0, top, jnp.where(row == 1, high, jnp.where(row == 2, total - high, 0.0)))
    return jnp.concatenate([values.astype(bf16), tail.astype(bf16)], axis=0)


def kernel(
    q_hbm, list_hbm, len_in, k_hbm, v_hbm, sk_hbm, sv_hbm, out_ref,
    q_in, list_in, k_in, v_in, sk_in, sv_in, qfmt, work,
    qbuf, kv, vsib, scores0, scores1, hide, eye, part, ra, rb, rc, fin, suf_o, suf_ml,
    send_sems, recv_sems, loc_sems,
):
    ctx = lax.axis_index("ctx")
    slab = lax.axis_index("slab")
    core = lax.rem(ctx, 2)
    z = lax.rem(ctx // 2, NZ)
    x = slab // 2
    y = lax.rem(slab, 2) * 2 + ctx // (2 * NZ)

    def device(x, y, z, core):
        return (lax.rem(y, 2) * NZ + z) * 2 + core, x * 2 + y // 2

    sib = device(x, y, z, 1 - core)
    xps = [device(lax.rem(x + 1, NX), y, z, c) for c in (core, 1 - core)]
    xms = [device(lax.rem(x + NX - 1, NX), y, z, c) for c in (core, 1 - core)]
    yp = device(x, lax.rem(y + 1, NY), z, core)
    ym = device(x, lax.rem(y + NY - 1, NY), z, core)
    along_z = [[device(x, y, lax.rem(z + dz, NZ), c) for dz in range(NZ)] for c in (core, 1 - core)]

    loads = []
    pairs = ((k_hbm, k_in), (v_hbm, v_in), (q_hbm, q_in), (list_hbm, list_in), (sk_hbm, sk_in), (sv_hbm, sv_in))
    for n, (src, dst) in enumerate(pairs):
        loads.append(pltpu.make_async_copy(src, dst, loc_sems.at[n]))
        loads[n].start()

    barrier = pltpu.get_barrier_semaphore()
    peers = [sib, *xps, *xms, yp, ym] + along_z[0][1:] + along_z[1][1:]
    for other in peers:
        pl.semaphore_signal(barrier, inc=1, device_id=other, device_id_type=pl.DeviceIdType.MESH)

    def own_kv(k):
        mine = pl.ds(pl.multiple_of(core * 256 + k * 128, 128), 128)
        theirs = pl.ds(pl.multiple_of((1 - core) * 256 + k * 128, 128), 128)
        for blk in range(2):
            vsib[k, 0, blk] = k_in[blk, :, theirs].T
            vsib[k, 1, blk] = v_in[blk, :, theirs]
            kv[k, 0, 0, 0, blk] = k_in[blk, :, mine].T
            kv[k, 0, 0, 1, blk] = v_in[blk, :, mine]

    loads[0].wait()
    loads[1].wait()
    own_kv(0)

    loads[2].wait()

    def queries(k):
        for half in range(2):
            for h in range(RATIO):
                col = ((half * 2 + k) * RATIO + h) * HEAD_DIM
                work[pl.ds(h * OWN, OWN), :] = q_in[:, col : col + HEAD_DIM].astype(f32)
            qfmt[half, k, 0:ROWS, :] = work[0:ROWS, :].astype(bf16)

    queries(0)
    loads[3].wait()
    lists = list_in[...]
    lane = lax.broadcasted_iota(jnp.int32, (OWN, 128), 1)
    seen = jnp.zeros((OWN, 128), f32)
    for n in range(lists.shape[1]):
        seen = jnp.where(lists[:, n : n + 1] == lane, 1.0, seen)
    work[0:16, :] = jnp.zeros((16, 128), f32)
    work[0:OWN, :] = seen
    for half in range(2):
        qfmt[half, 0, ROWS:QROWS, :] = work[0:16, :].astype(bf16)

    pl.semaphore_wait(barrier, len(peers))

    copies = {}
    done = set()

    def copy_of(name):
        n, src, dst, to = copies[name]
        return pltpu.make_async_remote_copy(
            src_ref=src, dst_ref=dst, send_sem=send_sems.at[n], recv_sem=recv_sems.at[n],
            device_id=to, device_id_type=pl.DeviceIdType.MESH,
        )

    def send(name, src, dst, to):
        copies[name] = (len(copies), src, dst, to)
        copy_of(name).start()

    def got(*name):
        if name not in done:
            done.add(name)
            copy_of(name).wait_recv()

    def kv_send(k):
        send(("kvsib", k), vsib.at[k], kv.at[k, 0, 1], sib)
        for c, src in enumerate((kv.at[k, 0, 0], vsib.at[k])):
            send(("kv1", k, c), src, kv.at[k, 1, c], xps[c])
            send(("kv2", k, c), src, kv.at[k, 2, c], xms[c])

    def kv_forward(k):
        got("kv1", k, 0)
        send(("kv3", k, 0), kv.at[k, 1, 0], kv.at[k, 3, 0], xps[0])
        got("kv2", k, 1)
        send(("kv3", k, 1), kv.at[k, 2, 1], kv.at[k, 3, 1], xms[0])

    def kv_last(k):
        got("kvsib", k)
        for c in range(2):
            for name in ("kv1", "kv2", "kv3"):
                got(name, k, c)

    def slot(k, dy, dz, which):
        rows = pl.ds(0, QROWS if k == 0 else ROWS)
        if which == 2:
            return qbuf.at[k, dy, place(dz), pl.ds(0, 2), rows]
        return qbuf.at[k, dy, place(dz), which, rows]

    def q_send(k):
        end = QROWS if k == 0 else ROWS
        qbuf[k, 0, place(0), 0, 0:end, :] = qfmt[core, k, 0:end, :]
        for to in (0, 1, 7, 2, 6, 3, 5, 4):
            for half in range(2):
                if to or half:
                    src = qfmt.at[core if half == 0 else 1 - core, k, pl.ds(0, end)]
                    send(("q", k, half, -to % NZ), src, slot(k, 0, -to, half), along_z[half][to])

    def y_send(k, *dzs):
        for dz in dzs:
            for half in range(2):
                if dz or half:
                    got("q", k, half, dz)
            send(("y3", k, dz), slot(k, 0, dz, 2), slot(k, 3, dz, 2), yp)
            send(("y1", k, dz), slot(k, 0, dz, 2), slot(k, 1, dz, 2), ym)

    def y_forward(k, *dzs):
        for dz in dzs:
            got("y3", k, dz)
            send(("y2a", k, dz), slot(k, 3, dz, 0), slot(k, 2, dz, 0), yp)
            got("y1", k, dz)
            send(("y2b", k, dz), slot(k, 1, dz, 1), slot(k, 2, dz, 1), ym)

    def y_last(k):
        for dz in range(NZ):
            got("y2a", k, dz)
            got("y2b", k, dz)

    def suffix(k):
        zero = jnp.zeros((ROWS, 128), bf16)
        s = None
        for half in range(2):
            which = core if half == 0 else 1 - core
            cols = pl.ds(pl.multiple_of(which * 256 + k * 128, 128), 128)
            q = qfmt[which, k, 0:ROWS, :]
            q = jnp.concatenate([q, zero] if half == 0 else [zero, q], axis=0)
            keys = sk_in[:, :, cols].reshape(1024, 128)
            more = lax.dot_general(keys, q, NT, preferred_element_type=f32)
            s = more if s is None else s + more
        token = lax.broadcasted_iota(jnp.int32, (1024, 128), 0)
        lane = lax.broadcasted_iota(jnp.int32, (1024, 128), 1)
        branch = lax.broadcasted_iota(jnp.int32, (1, 128), 1) & (OWN - 1)
        length = jnp.zeros((1, 128), jnp.int32)
        for b in range(OWN):
            length = jnp.where(branch == b, len_in[b], length)
        ok = ((token >> 8) == (lane & (OWN - 1))) & ((token & 255) < length)
        top = jnp.max(jnp.where(ok, s, NEG), axis=0, keepdims=True)
        w = jnp.where(ok, jnp.exp2((s - top) * EXP_SCALE), 0.0)
        total = jnp.sum(w, axis=0, keepdims=True)
        w = w.astype(bf16)
        both = []
        for half in range(2):
            which = core if half == 0 else 1 - core
            cols = pl.ds(pl.multiple_of(which * 256 + k * 128, 128), 128)
            values = sv_in[:, :, cols].reshape(1024, 128)
            both.append(lax.dot_general(values, w, TN, preferred_element_type=f32))
        lane = lax.broadcasted_iota(jnp.int32, (128, 128), 1)
        suf_o[k] = jnp.where(lane < ROWS, both[0], both[1])
        suf_ml[k, 0:1] = top
        suf_ml[k, 1:2] = total

    row = lax.broadcasted_iota(jnp.int32, (128, 128), 0)
    lane = lax.broadcasted_iota(jnp.int32, (128, 128), 1)
    block_id = jnp.where(lane < 2, 2 * ctx + lane, 2 * (ctx + 1 - 2 * core) + lane - 2)
    pick = ((row == block_id) & (lane < 4)).astype(f32).astype(bf16)
    row = lax.broadcasted_iota(jnp.int32, (TILE, 256), 0)
    lane = lax.broadcasted_iota(jnp.int32, (TILE, 256), 1)
    spread = ((lane >> 4) == (row >> 6)) & ((lane & 15) == (row & (OWN - 1)))
    spread = spread.astype(f32).astype(bf16)

    def constants():
        row = lax.broadcasted_iota(jnp.int32, (128, 128), 0)
        for j in range(4):
            hide[j] = jnp.where(row == j, NEG, 0.0).astype(bf16)
        row = lax.broadcasted_iota(jnp.int32, (PROWS, 256), 0)
        lane = lax.broadcasted_iota(jnp.int32, (PROWS, 256), 1)
        eye[...] = (row == lane).astype(f32).astype(bf16)

    class Tile:
        def __init__(self, n, k, dys, g):
            self.k, self.dys, self.g = k, dys, g
            self.scores = (scores0, scores1)[n % 2]

        def front(self, j):
            if j == 0:
                slots = slice(4 * self.g, 4 * self.g + 4)
                q = [qbuf[self.k, dy, slots, :, 0:ROWS, :].reshape(TILE // 2, 128) for dy in self.dys]
                q = jnp.concatenate(q, axis=0)
                bits = [qbuf[0, dy, slots, :, ROWS:QROWS, :].reshape(128, 128) for dy in self.dys]
                bits = jnp.concatenate(bits, axis=0)
                unseen = jnp.dot((1.0 - bits.astype(f32)).astype(bf16), pick, preferred_element_type=f32)
                unseen = jnp.dot(spread, unseen.astype(bf16), preferred_element_type=f32)
                self.q = jnp.concatenate([q, unseen.astype(bf16)], axis=1)
                self.top = jnp.full((TILE, 128), NEG, f32)
            keys = jnp.concatenate([kv[self.k, xs, j // 2, 0, j % 2] for xs in range(4)], axis=1)
            keys = jnp.concatenate([keys, jnp.concatenate([hide[j]] * 4, axis=1)], axis=0)
            s = jnp.dot(self.q, keys, preferred_element_type=f32)
            self.scores[:, pl.ds(j * 512, 512)] = s
            for c in range(0, 512, 128):
                self.top = jnp.maximum(self.top, s[:, c : c + 128])

        def back(self, j):
            if j == 0:
                top = jnp.max(self.top, axis=1, keepdims=True)
                self.top = jnp.maximum(top, 0.1 * NEG).astype(bf16).astype(f32)
                self.acc = jnp.zeros((TILE, 256), f32)
            values = jnp.concatenate([kv[self.k, xs, j // 2, 1, j % 2] for xs in range(4)], axis=0)
            values = jnp.concatenate([values, jnp.ones((512, 128), bf16)], axis=1)
            w = jnp.exp2((self.scores[:, pl.ds(j * 512, 512)] - self.top) * EXP_SCALE).astype(bf16)
            self.acc = self.acc + jnp.dot(w, values, preferred_element_type=f32)

        def store(self):
            total = self.acc[:, 128:]
            high = total.astype(bf16).astype(f32)
            lane = lax.broadcasted_iota(jnp.int32, (TILE, 128), 1)
            tail = jnp.where(lane == 0, self.top, jnp.where(lane == 1, high, jnp.where(lane == 2, total - high, 0.0)))
            packed = jnp.concatenate([self.acc[:, :128].astype(bf16), tail.astype(bf16)], axis=1)
            turned = lax.dot_general(eye[...], packed, NT, preferred_element_type=f32).astype(bf16)
            for i in range(8):
                part[self.k, self.dys[i // 4], 4 * self.g + i % 4] = turned[:, i * 128 : i * 128 + 128]

    def fold(pieces):
        total = pieces[0].astype(f32)
        row = lax.broadcasted_iota(jnp.int32, (16, 128), 0)
        for other in pieces[1:-1]:
            values, top, mass = combine(total, other.astype(f32))
            tail = jnp.where(row == 0, top, jnp.where(row == 1, mass, 0.0))
            total = jnp.concatenate([values, tail], axis=0)
        return combine(total, pieces[-1].astype(f32))

    def merge(k, dy, dz, *others):
        dz = place(dz)
        others = [buf[tuple(index)] for buf, *index in others]
        part[k, dy, dz] = pack(*fold([part[k, dy, dz]] + others))

    def y_reduce(k, g, step):
        dzs = [(4 * g + i - 1) % NZ for i in range(4)]
        a, b = pl.ds(4 * g, 2), pl.ds(4 * g + 2, 2)
        if step == 0:
            send(("ra", k, g), part.at[k, 2, a], ra.at[k, g], yp)
            send(("rb", k, g), part.at[k, 2, b], rb.at[k, g], ym)
            send(("rcb", k, g), part.at[k, 1, b], rc.at[k, 0, b], yp)
        elif step == 1:
            send(("rda", k, g), part.at[k, 3, a], rc.at[k, 1, a], ym)
            got("ra", k, g)
            for i in range(2):
                merge(k, 1, dzs[i], (ra, k, g, i))
            send(("rca", k, g), part.at[k, 1, a], rc.at[k, 0, a], yp)
            got("rb", k, g)
            for i in range(2):
                merge(k, 3, dzs[2 + i], (rb, k, g, i))
            send(("rdb", k, g), part.at[k, 3, b], rc.at[k, 1, b], ym)
        else:
            for name in ("rcb", "rda", "rca", "rdb"):
                got(name, k, g)
            for i in (1, 2, 0, 3) if g else (3, 0, 2, 1):
                merge(k, 0, dzs[i], (rc, k, 0, 4 * g + i), (rc, k, 1, 4 * g + i))

    def z_out(k, g):
        for dz in [(4 * g + i - 1) % NZ for i in range(4)]:
            for half in range(2):
                if dz or half:
                    send(("fin", k, half, dz), part.at[k, 0, place(dz)], fin.at[k, half, dz], along_z[half][dz])

    def finish(k):
        lane = lax.broadcasted_iota(jnp.int32, (PROWS, 128), 1)
        pieces = []
        for dz in range(NZ):
            for half in range(2):
                if dz or half:
                    got("fin", k, half, dz)
            first = fin[k, 0, dz] if dz else part[k, 0, place(0)]
            pieces.append(jnp.where(lane < ROWS, first.astype(f32), fin[k, 1, dz].astype(f32)))
        values, top_a, mass = fold(pieces)
        top_b = suf_ml[k, 0:1]
        top = jnp.maximum(top_a, top_b)
        fa = jnp.exp2((top_a - top) * EXP_SCALE)
        fb = jnp.exp2((top_b - top) * EXP_SCALE)
        total = mass * fa + suf_ml[k, 1:2] * fb
        work[...] = ((values * fa + suf_o[k] * fb) / total).T
        for half in range(2):
            which = core if half == 0 else 1 - core
            for h in range(RATIO):
                col = pl.multiple_of((which * 2 + k) * RATIO * HEAD_DIM + h * HEAD_DIM, 128)
                rows = work[pl.ds(half * ROWS + h * OWN, OWN), :]
                out_ref[:, pl.ds(col, HEAD_DIM)] = rows.astype(bf16)

    kv_send(0)
    q_send(0)
    own_kv(1)
    y_send(0, 0)
    queries(1)
    y_send(0, 1, 7, 2, 6)
    kv_forward(0)
    y_send(0, 3, 5, 4)
    kv_send(1)
    q_send(1)
    constants()
    y_forward(0, 0, 1, 7)
    loads[4].wait()
    loads[5].wait()
    suffix(0)
    y_forward(0, 2, 6, 3, 5, 4)
    kv_last(0)

    order = [(0, dys, g) for dys in ((0, 1), (3, 2)) for g in (0, 1)]
    order += [(1, dys, g) for g in (1, 0) for dys in ((2, 1), (3, 0))]
    events = {}

    def at(n, f, *args):
        events.setdefault(n, []).append((f, args))

    at(0, y_send, 1, 0, 1, 7)
    at(1, y_send, 1, 2, 6)
    at(1, kv_forward, 1)
    at(2, y_send, 1, 3, 5, 4)
    at(3, y_last, 0)
    at(5, y_forward, 1, 0, 1, 7, 2)
    at(7, y_forward, 1, 6, 3, 5, 4)
    at(11, kv_last, 1)
    at(11, y_last, 1)
    at(11, y_reduce, 0, 0, 0)
    at(15, y_reduce, 0, 0, 1)
    at(15, y_reduce, 0, 1, 0)
    at(18, y_reduce, 0, 0, 2)
    at(18, z_out, 0, 0)
    at(18, y_reduce, 0, 1, 1)
    at(22, y_reduce, 0, 1, 2)
    at(22, z_out, 0, 1)
    at(19, y_reduce, 1, 1, 0)
    at(23, y_reduce, 1, 1, 1)
    at(26, y_reduce, 1, 1, 2)
    at(26, z_out, 1, 1)
    at(27, y_reduce, 1, 0, 0)
    at(31, y_reduce, 1, 0, 1)
    at(31, suffix, 1)
    at(31, y_reduce, 1, 0, 2)
    at(31, z_out, 1, 0)
    at(31, finish, 0)
    at(31, finish, 1)

    tile = Tile(0, *order[0])
    for j in range(4):
        tile.front(j)
    for n in range(len(order)):
        following = Tile(n + 1, *order[n + 1]) if n + 1 < len(order) else None
        for j in range(4):
            if following is not None:
                following.front(j)
            tile.back(j)
            if j == 3:
                tile.store()
                tile = following
            for f, args in events.get(4 * n + j, []):
                f(*args)
    for name in copies:
        if name not in done:
            copy_of(name).wait_recv()
        copy_of(name).wait_send()


def shards(
    queries, block_lists, suffix_lengths, prompt_keys, prompt_values, suffix_keys, suffix_values
):
    hbm = pl.BlockSpec(memory_space=pltpu.HBM)
    vmem = pl.BlockSpec(memory_space=pltpu.VMEM)
    smem = pl.BlockSpec(memory_space=pltpu.SMEM)
    return pl.pallas_call(
        kernel,
        out_shape=jax.ShapeDtypeStruct(queries.shape, bf16),
        in_specs=[hbm, hbm, smem, hbm, hbm, hbm, hbm],
        out_specs=vmem,
        scratch_shapes=[
            pltpu.VMEM(queries.shape, bf16),
            pltpu.VMEM(block_lists.shape, jnp.int32),
            pltpu.VMEM(prompt_keys.shape, bf16),
            pltpu.VMEM(prompt_values.shape, bf16),
            pltpu.VMEM(suffix_keys.shape, bf16),
            pltpu.VMEM(suffix_values.shape, bf16),
            pltpu.VMEM((2, 2, QROWS, 128), bf16),
            pltpu.VMEM((128, 128), f32),
            pltpu.VMEM((2, NY, NZ, 2, QROWS, 128), bf16),
            pltpu.VMEM((2, 4, 2, 2, 2, 128, 128), bf16),
            pltpu.VMEM((2, 2, 2, 128, 128), bf16),
            pltpu.VMEM((TILE, 2048), f32),
            pltpu.VMEM((TILE, 2048), f32),
            pltpu.VMEM((4, 128, 128), bf16),
            pltpu.VMEM((PROWS, 256), bf16),
            pltpu.VMEM((2, NY, NZ, PROWS, 128), bf16),
            pltpu.VMEM((2, 2, 2, PROWS, 128), bf16),
            pltpu.VMEM((2, 2, 2, PROWS, 128), bf16),
            pltpu.VMEM((2, 2, NZ, PROWS, 128), bf16),
            pltpu.VMEM((2, 2, NZ, PROWS, 128), bf16),
            pltpu.VMEM((2, 128, 128), f32),
            pltpu.VMEM((2, 8, 128), f32),
            pltpu.SemaphoreType.DMA((COPIES,)),
            pltpu.SemaphoreType.DMA((COPIES,)),
            pltpu.SemaphoreType.DMA((6,)),
        ],
        compiler_params=pltpu.CompilerParams(
            collective_id=0, has_side_effects=True, vmem_limit_bytes=56 * 1024 * 1024
        ),
    )(queries, block_lists, suffix_lengths, prompt_keys, prompt_values, suffix_keys, suffix_values)


def solution(mesh):
    return jax.shard_map(
        shards,
        mesh=mesh,
        in_specs=(
            P(("ctx", "slab"), None),
            P(("ctx", "slab"), None),
            P(("ctx", "slab")),
            P("ctx", "slab", None),
            P("ctx", "slab", None),
            P(("ctx", "slab"), None, None),
            P(("ctx", "slab"), None, None),
        ),
        out_specs=P(("ctx", "slab"), None),
        check_vma=False,
    )
```

time: 95.5 us -> 81.4 us (0.85)
  Pallas kernels: 93.8 us -> 79.7 us
    pallas_call x1, Pallas kernels: 93.8 us -> 79.7 us  [shards(): pl.pallas_call(kernel, out_shape=jax.ShapeDtypeStruct(queries.shape, bf16...]
where the time goes in v4:
time: 81.4 us; the launch traced here: 81.2 us
  Pallas kernels  79.7 us (98%)
  local copies, waits for them, and re-layouts  1.49 us (2%)
    pallas_call x1, Pallas kernels, shards(): pl.pallas_call(kernel, out_shape=jax.ShapeDtypeStruct(queries.shape, bf16...  79.7 us

profile of v4, /device:TPU:1, one launch (start us, length us, event | category | flops | bytes accessed | tf_op | source)
XLA Modules:
  0.0 81.2 jit_solution(12479789564572909371)
XLA Ops:
  0.0 79.7 %shard_map.73 = bf16[4,8192]{1,0:T(4,128)(2,1)} custom-call(bf16[4,8192]{1,0:T(4,128)(2,1)} %q_hbm.1, s32[4,32]{1,0:T(4,128)} %list_hbm.1, s32[4]{0:T(128)} %len_in.1, bf16[2,128,512]{2,1,0:T(8,128)(2,1)} %k_hbm.1, bf16[2,128,512]{2,1,0:T(8,128)(2,1)} %v_hbm.1, bf16[4,256,512]{2,1,0:T(8,128)(2,1)} %sk_hbm.1, bf16[4,256,512]{2,1,0:T(8,128)(2,1)} %sv_hbm.1), custom_call_target="tpu_custom_call" | custom-call | tf_op jit(solution)/shard_map/pallas_call | solution.py:432
  79.8 1.5 %copy.9 = bf16[4,8192]{1,0:T(4,128)(2,1)} copy(bf16[4,8192]{1,0:T(4,128)(2,1)} %shard_map.73) | data formatting | bytes 131072

commit v5 on v4

--- a/solution.py
+++ b/solution.py
@@ -170,25 +170,30 @@
                     src = qfmt.at[core if half == 0 else 1 - core, k, pl.ds(0, end)]
                     send(("q", k, half, -to % NZ), src, slot(k, 0, -to, half), along_z[half][to])
 
-    def y_send(k, *dzs):
-        for dz in dzs:
+    def group(k, dy, g, which):
+        rows = pl.ds(0, QROWS if k == 0 else ROWS)
+        if which == 2:
+            return qbuf.at[k, dy, pl.ds(4 * g, 4), pl.ds(0, 2), rows]
+        return qbuf.at[k, dy, pl.ds(4 * g, 4), which, rows]
+
+    def y_send(k, g):
+        for dz in ((0, 1, 7, 2), (6, 3, 5, 4))[g]:
             for half in range(2):
                 if dz or half:
                     got("q", k, half, dz)
-            send(("y3", k, dz), slot(k, 0, dz, 2), slot(k, 3, dz, 2), yp)
-            send(("y1", k, dz), slot(k, 0, dz, 2), slot(k, 1, dz, 2), ym)
-
-    def y_forward(k, *dzs):
-        for dz in dzs:
-            got("y3", k, dz)
-            send(("y2a", k, dz), slot(k, 3, dz, 0), slot(k, 2, dz, 0), yp)
-            got("y1", k, dz)
-            send(("y2b", k, dz), slot(k, 1, dz, 1), slot(k, 2, dz, 1), ym)
+        send(("y3", k, g), group(k, 0, g, 2), group(k, 3, g, 2), yp)
+        send(("y1", k, g), group(k, 0, g, 2), group(k, 1, g, 2), ym)
+
+    def y_forward(k, g):
+        got("y3", k, g)
+        send(("y2a", k, g), group(k, 3, g, 0), group(k, 2, g, 0), yp)
+        got("y1", k, g)
+        send(("y2b", k, g), group(k, 1, g, 1), group(k, 2, g, 1), ym)
 
     def y_last(k):
-        for dz in range(NZ):
-            got("y2a", k, dz)
-            got("y2b", k, dz)
+        for g in range(2):
+            got("y2a", k, g)
+            got("y2b", k, g)
 
     def suffix(k):
         zero = jnp.zeros((ROWS, 128), bf16)
@@ -344,27 +349,24 @@
         work[...] = ((values * fa + suf_o[k] * fb) / total).T
         for half in range(2):
             which = core if half == 0 else 1 - core
-            for h in range(RATIO):
-                col = pl.multiple_of((which * 2 + k) * RATIO * HEAD_DIM + h * HEAD_DIM, 128)
-                rows = work[pl.ds(half * ROWS + h * OWN, OWN), :]
-                out_ref[:, pl.ds(col, HEAD_DIM)] = rows.astype(bf16)
+            for b in range(OWN):
+                rows = work[pl.ds(half * ROWS + b, RATIO, stride=OWN), :]
+                out_ref[b, which * 2 + k] = rows.astype(bf16)
 
     kv_send(0)
     q_send(0)
     own_kv(1)
     y_send(0, 0)
     queries(1)
-    y_send(0, 1, 7, 2, 6)
     kv_forward(0)
-    y_send(0, 3, 5, 4)
+    y_send(0, 1)
     kv_send(1)
     q_send(1)
     constants()
-    y_forward(0, 0, 1, 7)
+    y_forward(0, 0)
     loads[4].wait()
     loads[5].wait()
     suffix(0)
-    y_forward(0, 2, 6, 3, 5, 4)
     kv_last(0)
 
     order = [(0, dys, g) for dys in ((0, 1), (3, 2)) for g in (0, 1)]
@@ -374,13 +376,12 @@
     def at(n, f, *args):
         events.setdefault(n, []).append((f, args))
 
-    at(0, y_send, 1, 0, 1, 7)
-    at(1, y_send, 1, 2, 6)
+    at(0, y_send, 1, 0)
     at(1, kv_forward, 1)
-    at(2, y_send, 1, 3, 5, 4)
+    at(2, y_send, 1, 1)
     at(3, y_last, 0)
-    at(5, y_forward, 1, 0, 1, 7, 2)
-    at(7, y_forward, 1, 6, 3, 5, 4)
+    at(5, y_forward, 1, 0)
+    at(7, y_forward, 1, 1)
     at(11, kv_last, 1)
     at(11, y_last, 1)
     at(11, y_reduce, 0, 0, 0)
@@ -406,6 +407,7 @@
     tile = Tile(0, *order[0])
     for j in range(4):
         tile.front(j)
+    y_forward(0, 1)
     for n in range(len(order)):
         following = Tile(n + 1, *order[n + 1]) if n + 1 < len(order) else None
         for j in range(4):
@@ -429,9 +431,9 @@
     hbm = pl.BlockSpec(memory_space=pltpu.HBM)
     vmem = pl.BlockSpec(memory_space=pltpu.VMEM)
     smem = pl.BlockSpec(memory_space=pltpu.SMEM)
-    return pl.pallas_call(
+    out = pl.pallas_call(
         kernel,
-        out_shape=jax.ShapeDtypeStruct(queries.shape, bf16),
+        out_shape=jax.ShapeDtypeStruct((OWN, KV_HEADS, RATIO, HEAD_DIM), bf16),
         in_specs=[hbm, hbm, smem, hbm, hbm, hbm, hbm],
         out_specs=vmem,
         scratch_shapes=[
@@ -465,6 +467,7 @@
             collective_id=0, has_side_effects=True, vmem_limit_bytes=56 * 1024 * 1024
         ),
     )(queries, block_lists, suffix_lengths, prompt_keys, prompt_values, suffix_keys, suffix_values)
+    return out.reshape(queries.shape)
 
 
 def solution(mesh):

time: 81.4 us -> 82.5 us (1.014)
  Pallas kernels: 79.7 us -> 80.8 us
    pallas_call x1, Pallas kernels: 79.7 us -> 80.8 us  [shards(): pl.pallas_call(kernel, out_shape=jax.ShapeDtypeStruct((OWN, KV_HEADS, RAT...]
where the time goes in v5:
time: 82.5 us; the launch traced here: 82.3 us
  Pallas kernels  80.8 us (98%)
  local copies, waits for them, and re-layouts  1.52 us (2%)
    pallas_call x1, Pallas kernels, shards(): pl.pallas_call(kernel, out_shape=jax.ShapeDtypeStruct((OWN, KV_HEADS, RAT...  80.8 us

profile of v5, /device:TPU:1, one launch (start us, length us, event | category | flops | bytes accessed | tf_op | source)
XLA Modules:
  0.0 82.3 jit_solution(9585969736863764529)
XLA Ops:
  0.0 80.8 %shard_map.73 = bf16[4,4,16,128]{3,2,1,0:T(8,128)(2,1)} custom-call(bf16[4,8192]{1,0:T(4,128)(2,1)} %q_hbm.1, s32[4,32]{1,0:T(4,128)} %list_hbm.1, s32[4]{0:T(128)} %len_in.1, bf16[2,128,512]{2,1,0:T(8,128)(2,1)} %k_hbm.1, bf16[2,128,512]{2,1,0:T(8,128)(2,1)} %v_hbm.1, bf16[4,256,512]{2,1,0:T(8,128)(2,1)} %sk_hbm.1, bf16[4,256,512]{2,1,0:T(8,128)(2,1)} %sv_hbm.1), custom_call_target="tpu_custom_call" | custom-call | tf_op jit(solution)/shard_map/pallas_call | solution.py:434
  80.8 1.5 %copy.10 = bf16[1,4,64,128]{3,1,2,0:T(4,128)(2,1)} copy(bf16[1,4,64,128]{3,2,1,0:T(8,128)(2,1)} %bitcast.5) | data formatting | bytes 131072

commit v6 on v4

--- a/solution.py
+++ b/solution.py
@@ -352,19 +352,18 @@
     kv_send(0)
     q_send(0)
     own_kv(1)
-    y_send(0, 0)
-    queries(1)
-    y_send(0, 1, 7, 2, 6)
+    y_send(0, 0, 1, 7, 2, 6)
     kv_forward(0)
     y_send(0, 3, 5, 4)
+    y_forward(0, 0, 1, 7)
+    queries(1)
     kv_send(1)
     q_send(1)
     constants()
-    y_forward(0, 0, 1, 7)
+    y_forward(0, 2, 6)
     loads[4].wait()
     loads[5].wait()
     suffix(0)
-    y_forward(0, 2, 6, 3, 5, 4)
     kv_last(0)
 
     order = [(0, dys, g) for dys in ((0, 1), (3, 2)) for g in (0, 1)]
@@ -406,6 +405,8 @@
     tile = Tile(0, *order[0])
     for j in range(4):
         tile.front(j)
+        if j % 2:
+            y_forward(0, *((3, 5), (4,))[j // 2])
     for n in range(len(order)):
         following = Tile(n + 1, *order[n + 1]) if n + 1 < len(order) else None
         for j in range(4):

time: 81.4 us -> 81.7 us (level)
  no operation moved by 1% of the time
where the time goes in v6:
time: 81.7 us; the launch traced here: 81.5 us
  Pallas kernels  80 us (98%)
  local copies, waits for them, and re-layouts  1.49 us (2%)
    pallas_call x1, Pallas kernels, shards(): pl.pallas_call(kernel, out_shape=jax.ShapeDtypeStruct(queries.shape, bf16...  80 us

profile of v6, /device:TPU:1, one launch (start us, length us, event | category | flops | bytes accessed | tf_op | source)
XLA Modules:
  0.0 81.5 jit_solution(9961916937329756340)
XLA Ops:
  0.0 80.0 %shard_map.73 = bf16[4,8192]{1,0:T(4,128)(2,1)} custom-call(bf16[4,8192]{1,0:T(4,128)(2,1)} %q_hbm.1, s32[4,32]{1,0:T(4,128)} %list_hbm.1, s32[4]{0:T(128)} %len_in.1, bf16[2,128,512]{2,1,0:T(8,128)(2,1)} %k_hbm.1, bf16[2,128,512]{2,1,0:T(8,128)(2,1)} %v_hbm.1, bf16[4,256,512]{2,1,0:T(8,128)(2,1)} %sk_hbm.1, bf16[4,256,512]{2,1,0:T(8,128)(2,1)} %sv_hbm.1), custom_call_target="tpu_custom_call" | custom-call | tf_op jit(solution)/shard_map/pallas_call | solution.py:433
  80.1 1.5 %copy.9 = bf16[4,8192]{1,0:T(4,128)(2,1)} copy(bf16[4,8192]{1,0:T(4,128)(2,1)} %shard_map.73) | data formatting | bytes 131072

commit v7 on v4

--- a/solution.py
+++ b/solution.py
@@ -138,22 +138,23 @@
             copy_of(name).wait_recv()
 
     def kv_send(k):
-        send(("kvsib", k), vsib.at[k], kv.at[k, 0, 1], sib)
-        for c, src in enumerate((kv.at[k, 0, 0], vsib.at[k])):
-            send(("kv1", k, c), src, kv.at[k, 1, c], xps[c])
-            send(("kv2", k, c), src, kv.at[k, 2, c], xms[c])
-
-    def kv_forward(k):
-        got("kv1", k, 0)
-        send(("kv3", k, 0), kv.at[k, 1, 0], kv.at[k, 3, 0], xps[0])
-        got("kv2", k, 1)
-        send(("kv3", k, 1), kv.at[k, 2, 1], kv.at[k, 3, 1], xms[0])
-
-    def kv_last(k):
-        got("kvsib", k)
+        for i in range(2):
+            send(("kvsib", k, i), vsib.at[k, i], kv.at[k, 0, 1, i], sib)
+            for c, src in enumerate((kv.at[k, 0, 0, i], vsib.at[k, i])):
+                send(("kv1", k, c, i), src, kv.at[k, 1, c, i], xps[c])
+                send(("kv2", k, c, i), src, kv.at[k, 2, c, i], xms[c])
+
+    def kv_forward(k, i):
+        got("kv1", k, 0, i)
+        send(("kv3", k, 0, i), kv.at[k, 1, 0, i], kv.at[k, 3, 0, i], xps[0])
+        got("kv2", k, 1, i)
+        send(("kv3", k, 1, i), kv.at[k, 2, 1, i], kv.at[k, 3, 1, i], xms[0])
+
+    def kv_last(k, i):
+        got("kvsib", k, i)
         for c in range(2):
             for name in ("kv1", "kv2", "kv3"):
-                got(name, k, c)
+                got(name, k, c, i)
 
     def slot(k, dy, dz, which):
         rows = pl.ds(0, QROWS if k == 0 else ROWS)
@@ -353,19 +354,18 @@
     q_send(0)
     own_kv(1)
     y_send(0, 0)
+    kv_forward(0, 0)
     queries(1)
     y_send(0, 1, 7, 2, 6)
-    kv_forward(0)
+    kv_forward(0, 1)
     y_send(0, 3, 5, 4)
     kv_send(1)
     q_send(1)
     constants()
-    y_forward(0, 0, 1, 7)
+    y_forward(0, 0, 1, 7, 2)
     loads[4].wait()
     loads[5].wait()
-    suffix(0)
-    y_forward(0, 2, 6, 3, 5, 4)
-    kv_last(0)
+    kv_last(0, 0)
 
     order = [(0, dys, g) for dys in ((0, 1), (3, 2)) for g in (0, 1)]
     order += [(1, dys, g) for g in (1, 0) for dys in ((2, 1), (3, 0))]
@@ -376,12 +376,14 @@
 
     at(0, y_send, 1, 0, 1, 7)
     at(1, y_send, 1, 2, 6)
-    at(1, kv_forward, 1)
+    at(1, kv_forward, 1, 0)
+    at(2, kv_forward, 1, 1)
     at(2, y_send, 1, 3, 5, 4)
     at(3, y_last, 0)
     at(5, y_forward, 1, 0, 1, 7, 2)
     at(7, y_forward, 1, 6, 3, 5, 4)
-    at(11, kv_last, 1)
+    at(11, kv_last, 1, 0)
+    at(11, kv_last, 1, 1)
     at(11, y_last, 1)
     at(11, y_reduce, 0, 0, 0)
     at(15, y_reduce, 0, 0, 1)
@@ -397,15 +399,20 @@
     at(26, z_out, 1, 1)
     at(27, y_reduce, 1, 0, 0)
     at(31, y_reduce, 1, 0, 1)
-    at(31, suffix, 1)
+    at(31, suffix, 0)
     at(31, y_reduce, 1, 0, 2)
     at(31, z_out, 1, 0)
+    at(31, suffix, 1)
     at(31, finish, 0)
     at(31, finish, 1)
 
     tile = Tile(0, *order[0])
     for j in range(4):
         tile.front(j)
+        if j == 1:
+            y_forward(0, 6, 3)
+    y_forward(0, 5, 4)
+    kv_last(0, 1)
     for n in range(len(order)):
         following = Tile(n + 1, *order[n + 1]) if n + 1 < len(order) else None
         for j in range(4):

time: 81.4 us -> 81.2 us (level)
  no operation moved by 1% of the time
where the time goes in v7:
time: 81.2 us; the launch traced here: 81 us
  Pallas kernels  79.5 us (98%)
  local copies, waits for them, and re-layouts  1.49 us (2%)
    pallas_call x1, Pallas kernels, shards(): pl.pallas_call(kernel, out_shape=jax.ShapeDtypeStruct(queries.shape, bf16...  79.5 us

profile of v7, /device:TPU:1, one launch (start us, length us, event | category | flops | bytes accessed | tf_op | source)
XLA Modules:
  0.0 81.0 jit_solution(6213460475466357552)
XLA Ops:
  0.0 79.5 %shard_map.73 = bf16[4,8192]{1,0:T(4,128)(2,1)} custom-call(bf16[4,8192]{1,0:T(4,128)(2,1)} %q_hbm.1, s32[4,32]{1,0:T(4,128)} %list_hbm.1, s32[4]{0:T(128)} %len_in.1, bf16[2,128,512]{2,1,0:T(8,128)(2,1)} %k_hbm.1, bf16[2,128,512]{2,1,0:T(8,128)(2,1)} %v_hbm.1, bf16[4,256,512]{2,1,0:T(8,128)(2,1)} %sk_hbm.1, bf16[4,256,512]{2,1,0:T(8,128)(2,1)} %sv_hbm.1), custom_call_target="tpu_custom_call" | custom-call | tf_op jit(solution)/shard_map/pallas_call | solution.py:439
  79.5 1.5 %copy.9 = bf16[4,8192]{1,0:T(4,128)(2,1)} copy(bf16[4,8192]{1,0:T(4,128)(2,1)} %shard_map.73) | data formatting | bytes 131072
